TPU v7x, 32 devices: a whole 2x2x4 slice. The times are simulated.
32 devices in a mesh: seq: 16 (over z, y, core), head: 2 (over x).
Axes of the slice: x: 2, y: 2, z: 4, core: 2. Of those that a mesh axis runs over, the one named last changes fastest.
Arguments:
- tokens: bfloat16 [65536, 1024], P(('seq', 'head')), may hold values from -32 to 32
- w_qkv: bfloat16 [1024, 3072], P('seq'), may hold values from -0.1875 to 0.1875
- w_out: bfloat16 [1024, 1024], P('seq'), may hold values from -0.1875 to 0.1875
- neighbours: int32 [512, 12], P('seq'), may hold values from 0 to 511, as said below
Outputs:
- update: bfloat16 [65536, 1024], P(('seq', 'head'))
Inputs may be any that keep to these rules, and one draw needn't show every extreme that they name: Block b has grid coordinates z = b // 16, y = (b // 4) % 4, x = b % 4. Each row lists b itself first, then 11 different blocks among its 26 neighbours at offsets -1, 0, 1 in each coordinate (z taken modulo 512 // 16, y and x modulo 4).
All inputs are finite; a program needn't handle non-finite values.
Results may differ from a plain program's by a relative error of at most 0.0065.
The roundings to bfloat16 on the way count: a program that leaves them out, or rounds other values in their place, can miss the bound.
Values may be sent and summed in bfloat16 or wider, within the bound.
No kernel may reach another device: no remote copies, remote signals or barrier semaphores. Data moves between devices by JAX's collectives and lax.ppermute only.
A program may use at most 128 MiB of HBM per device.

v0:
```python
import math

import jax
import jax.numpy as jnp
from jax import lax
from jax.sharding import PartitionSpec as P

HEADS = 8
HD = 128
BLK = 128
NBR = 12
PB = 16


def padded_2(cells, sides, width):
    for axis, dim in sides:
        count = lax.axis_size(axis)
        head = lax.slice_in_dim(cells, 0, width, axis=dim)
        tail = lax.slice_in_dim(cells, cells.shape[dim] - width, cells.shape[dim], axis=dim)
        cells = jnp.concatenate(
            [
                lax.ppermute(tail, axis, [(i, (i + 1) % count) for i in range(count)]),
                cells,
                lax.ppermute(head, axis, [((i + 1) % count, i) for i in range(count)]),
            ],
            axis=dim,
        )
    return cells


def local(tokens, w_qkv, w_out, neighbours):
    head_count = lax.axis_size("head")
    seq_count = lax.axis_size("seq")
    per_device = HEADS // head_count
    local_rows = tokens.shape[0]
    slab_rows = local_rows * head_count
    full_qkv = lax.all_gather(w_qkv, "seq", axis=0, tiled=True)
    projected = jnp.dot(tokens, full_qkv, preferred_element_type=jnp.float32)
    projected = projected.astype(jnp.bfloat16).reshape(local_rows, 3, HEADS, HD)
    slab = lax.all_to_all(projected, "head", split_axis=2, concat_axis=0, tiled=True)
    queries = slab[:, 0]
    key_value = slab[:, 1:3]
    padded = padded_2(key_value, (("seq", 0),), PB * BLK)
    kv_blocks = padded.reshape(-1, BLK, 2, per_device, HD)
    block_count = neighbours.shape[0]
    first_block = lax.axis_index("seq") * block_count
    local_lists = jnp.mod(neighbours - first_block + PB, block_count * seq_count)
    group_blocks = 4
    scale = 1.0 / math.sqrt(HD)

    def attend(args):
        query_group, list_group = args
        picked = kv_blocks[list_group].reshape(group_blocks, NBR * BLK, 2, per_device, HD)
        keys = picked[:, :, 0]
        values = picked[:, :, 1]
        scores = (
            jnp.einsum("nqhd,nkhd->nhqk", query_group, keys, preferred_element_type=jnp.float32)
            * scale
        )
        largest = jnp.max(scores, axis=-1, keepdims=True)
        expo = jnp.exp(scores - largest)
        probs = (expo / jnp.sum(expo, axis=-1, keepdims=True)).astype(jnp.bfloat16)
        result = jnp.einsum("nhqk,nkhd->nqhd", probs, values, preferred_element_type=jnp.float32)
        return result.astype(jnp.bfloat16)

    grouped_q = queries.reshape(block_count // group_blocks, group_blocks, BLK, per_device, HD)
    grouped_l = local_lists.reshape(block_count // group_blocks, group_blocks, NBR)
    attended = lax.map(attend, (grouped_q, grouped_l)).reshape(slab_rows, per_device, HD)
    returned = lax.all_to_all(attended, "head", split_axis=0, concat_axis=1, tiled=True)
    flat = returned.reshape(local_rows, HEADS * HD)
    full_out = lax.all_gather(w_out, "seq", axis=0, tiled=True)
    update = jnp.dot(flat, full_out, preferred_element_type=jnp.float32)
    return update.astype(jnp.bfloat16)


def solution(mesh):
    return jax.shard_map(
        local,
        mesh=mesh,
        in_specs=(P(("seq", "head"), None), P("seq", None), P("seq", None), P("seq", None)),
        out_specs=P(("seq", "head"), None),
        check_vma=False,
    )
```

profile of v0, /device:TPU:1, one launch (start us, length us, event | category | flops | bytes accessed | tf_op | source)
XLA Modules:
  0.0 943.8 jit_solution(2801608497499605297)
XLA Ops:
  7.3 66.7 %all-gather.3.cloned.1.call-done = bf16[1024,3072]{1,0:T(8,128)(2,1)} async-done(((bf16[64,3072]{1,0:T(8,128)(2,1)}), bf16[1024,3072]{1,0:T(8,128)(2,1)}) %all-gather.3.cloned.1.call-update) | async-done | bytes 6291472 | tf_op jit(solution)/shard_map/all_gather | solution.py:37
  74.0 16.5 %convert_bitcast_fusion = bf16[256,8,24,128]{3,1,2,0:T(8,128)(2,1)S(1)} fusion(bf16[2048,1024]{1,0:T(8,128)(2,1)} %param.6, bf16[1024,3072]{1,0:T(8,128)(2,1)} %all-gather.3.cloned.1.call-done), kind=kOutput, calls=%fused_computation.20 | convolution fusion | flops 12891193344 | bytes 23068672 | tf_op jit(solution)/shard_map/dot_general | solution.py:38
  93.7 14.4 %copy.51 = bf16[2048,3,8,128]{3,0,1,2:T(8,128)(2,1)S(1)} copy(bf16[2048,3,8,128]{3,2,1,0:T(8,128)(2,1)S(1)} %bitcast.59) | data formatting | bytes 25165824 | tf_op jit(solution)/shard_map/reshape | solution.py:39
  108.1 140.5 %all_to_all.33 = bf16[2048,3,8,128]{3,0,1,2:T(8,128)(2,1)S(1)} all-to-all(bf16[2048,3,8,128]{3,0,1,2:T(8,128)(2,1)S(1)} %copy.51), channel_id=1, replica_groups=mesh['seq'=16,'head'=2] {'head'}, dimensions={2} | all-to-all | bytes 25165824 | tf_op jit(solution)/shard_map/all_to_all | solution.py:40
  271.4 85.6 %collective-permute-done = bf16[2048,2,4,128]{3,0,2,1:T(8,128)(2,1)} collective-permute-done((bf16[2048,2,4,128]{3,0,2,1:T(8,128)(2,1)}, bf16[2048,2,4,128]{3,0,2,1:T(8,128)(2,1)}, u32[]{:S(2)}, u32[]{:S(2)}) %collective-permute-start) | collective-permute-done | bytes 4194336 | tf_op jit(solution)/shard_map/ppermute | solution.py:22
  371.9 513.2 %while.10 = (s32[]{:T(128)}, bf16[8,4,128,4,128]{4,2,1,0,3:T(8,128)(2,1)}, s32[8,4,12]{2,1,0:T(4,128)S(1)}, bf16[64,128,2,4,128]{4,1,3,2,0:T(8,128)(2,1)}, bf16[8,4,128,4,128]{4,2,1,0,3:T(8,128)(2,1)}, /*index=5*/s32[]{:T(128)}) while((s32[]{:T(128)}, bf16[8,4,128,4,128]{4,2,1,0,3:T(8,128)(2,1)}, s32[8,4,12]{2,1,0:T(4,128)S(1)}, ...), condition=%wide.region_3.4_spmd, body=%wide.region_0.3_spmd.sunk | while | flops 1629751936 | bytes 154163408 | solution.py:68
  372.0 12.1 %gather_fusion = bf16[48,128,2,4,128]{4,1,3,2,0:T(8,128)(2,1)} fusion(bf16[64,128,2,4,128]{4,1,3,2,0:T(8,128)(2,1)} %get-tuple-element.128, s32[1024]{0:T(1024)S(1)} %pad_clamp_fusion.2), kind=kCustom, calls=%fused_computation.clone.1 | custom fusion | bytes 25166016 | tf_op jit(solution)/shard_map/while/body/eval_jaxpr/gather | solution.py:53
  402.1 15.7 %fusion.31 = (f32[4,4,128]{2,1,0:T(4,128)S(1)}, f32[4,4,128,1536]{3,2,1,0:T(8,128)}) fusion(f32[4,4,128,1536]{3,2,1,0:T(8,128)} %fusion.30), kind=kOutput, calls=%fused_computation.27.clone.1 | output fusion | flops 12584447 | bytes 25174016 | tf_op jit(solution)/shard_map/while/body/eval_jaxpr/sub | solution.py:61
  417.9 8.7 copy.77
  436.1 12.0 %gather_fusion = bf16[48,128,2,4,128]{4,1,3,2,0:T(8,128)(2,1)} fusion(bf16[64,128,2,4,128]{4,1,3,2,0:T(8,128)(2,1)} %get-tuple-element.128, s32[1024]{0:T(1024)S(1)} %pad_clamp_fusion.2), kind=kCustom, calls=%fused_computation.clone.1 | custom fusion | bytes 25166016 | tf_op jit(solution)/shard_map/while/body/eval_jaxpr/gather | solution.py:53
  466.3 15.7 %fusion.31 = (f32[4,4,128]{2,1,0:T(4,128)S(1)}, f32[4,4,128,1536]{3,2,1,0:T(8,128)}) fusion(f32[4,4,128,1536]{3,2,1,0:T(8,128)} %fusion.30), kind=kOutput, calls=%fused_computation.27.clone.1 | output fusion | flops 12584447 | bytes 25174016 | tf_op jit(solution)/shard_map/while/body/eval_jaxpr/sub | solution.py:61
  482.0 8.7 copy.77
  500.2 12.1 %gather_fusion = bf16[48,128,2,4,128]{4,1,3,2,0:T(8,128)(2,1)} fusion(bf16[64,128,2,4,128]{4,1,3,2,0:T(8,128)(2,1)} %get-tuple-element.128, s32[1024]{0:T(1024)S(1)} %pad_clamp_fusion.2), kind=kCustom, calls=%fused_computation.clone.1 | custom fusion | bytes 25166016 | tf_op jit(solution)/shard_map/while/body/eval_jaxpr/gather | solution.py:53
  530.4 15.7 %fusion.31 = (f32[4,4,128]{2,1,0:T(4,128)S(1)}, f32[4,4,128,1536]{3,2,1,0:T(8,128)}) fusion(f32[4,4,128,1536]{3,2,1,0:T(8,128)} %fusion.30), kind=kOutput, calls=%fused_computation.27.clone.1 | output fusion | flops 12584447 | bytes 25174016 | tf_op jit(solution)/shard_map/while/body/eval_jaxpr/sub | solution.py:61
  546.1 8.7 copy.77
  564.4 12.1 %gather_fusion = bf16[48,128,2,4,128]{4,1,3,2,0:T(8,128)(2,1)} fusion(bf16[64,128,2,4,128]{4,1,3,2,0:T(8,128)(2,1)} %get-tuple-element.128, s32[1024]{0:T(1024)S(1)} %pad_clamp_fusion.2), kind=kCustom, calls=%fused_computation.clone.1 | custom fusion | bytes 25166016 | tf_op jit(solution)/shard_map/while/body/eval_jaxpr/gather | solution.py:53
  594.6 15.7 %fusion.31 = (f32[4,4,128]{2,1,0:T(4,128)S(1)}, f32[4,4,128,1536]{3,2,1,0:T(8,128)}) fusion(f32[4,4,128,1536]{3,2,1,0:T(8,128)} %fusion.30), kind=kOutput, calls=%fused_computation.27.clone.1 | output fusion | flops 12584447 | bytes 25174016 | tf_op jit(solution)/shard_map/while/body/eval_jaxpr/sub | solution.py:61
  610.3 8.7 copy.77
  628.5 12.1 %gather_fusion = bf16[48,128,2,4,128]{4,1,3,2,0:T(8,128)(2,1)} fusion(bf16[64,128,2,4,128]{4,1,3,2,0:T(8,128)(2,1)} %get-tuple-element.128, s32[1024]{0:T(1024)S(1)} %pad_clamp_fusion.2), kind=kCustom, calls=%fused_computation.clone.1 | custom fusion | bytes 25166016 | tf_op jit(solution)/shard_map/while/body/eval_jaxpr/gather | solution.py:53
  658.7 15.7 %fusion.31 = (f32[4,4,128]{2,1,0:T(4,128)S(1)}, f32[4,4,128,1536]{3,2,1,0:T(8,128)}) fusion(f32[4,4,128,1536]{3,2,1,0:T(8,128)} %fusion.30), kind=kOutput, calls=%fused_computation.27.clone.1 | output fusion | flops 12584447 | bytes 25174016 | tf_op jit(solution)/shard_map/while/body/eval_jaxpr/sub | solution.py:61
  674.5 8.7 copy.77
  692.7 12.0 %gather_fusion = bf16[48,128,2,4,128]{4,1,3,2,0:T(8,128)(2,1)} fusion(bf16[64,128,2,4,128]{4,1,3,2,0:T(8,128)(2,1)} %get-tuple-element.128, s32[1024]{0:T(1024)S(1)} %pad_clamp_fusion.2), kind=kCustom, calls=%fused_computation.clone.1 | custom fusion | bytes 25166016 | tf_op jit(solution)/shard_map/while/body/eval_jaxpr/gather | solution.py:53
  722.9 15.7 %fusion.31 = (f32[4,4,128]{2,1,0:T(4,128)S(1)}, f32[4,4,128,1536]{3,2,1,0:T(8,128)}) fusion(f32[4,4,128,1536]{3,2,1,0:T(8,128)} %fusion.30), kind=kOutput, calls=%fused_computation.27.clone.1 | output fusion | flops 12584447 | bytes 25174016 | tf_op jit(solution)/shard_map/while/body/eval_jaxpr/sub | solution.py:61
  738.6 8.7 copy.77
  756.8 12.1 %gather_fusion = bf16[48,128,2,4,128]{4,1,3,2,0:T(8,128)(2,1)} fusion(bf16[64,128,2,4,128]{4,1,3,2,0:T(8,128)(2,1)} %get-tuple-element.128, s32[1024]{0:T(1024)S(1)} %pad_clamp_fusion.2), kind=kCustom, calls=%fused_computation.clone.1 | custom fusion | bytes 25166016 | tf_op jit(solution)/shard_map/while/body/eval_jaxpr/gather | solution.py:53
  787.0 15.7 %fusion.31 = (f32[4,4,128]{2,1,0:T(4,128)S(1)}, f32[4,4,128,1536]{3,2,1,0:T(8,128)}) fusion(f32[4,4,128,1536]{3,2,1,0:T(8,128)} %fusion.30), kind=kOutput, calls=%fused_computation.27.clone.1 | output fusion | flops 12584447 | bytes 25174016 | tf_op jit(solution)/shard_map/while/body/eval_jaxpr/sub | solution.py:61
  802.8 8.7 copy.77
  821.0 12.1 %gather_fusion = bf16[48,128,2,4,128]{4,1,3,2,0:T(8,128)(2,1)} fusion(bf16[64,128,2,4,128]{4,1,3,2,0:T(8,128)(2,1)} %get-tuple-element.128, s32[1024]{0:T(1024)S(1)} %pad_clamp_fusion.2), kind=kCustom, calls=%fused_computation.clone.1 | custom fusion | bytes 25166016 | tf_op jit(solution)/shard_map/while/body/eval_jaxpr/gather | solution.py:53
  851.2 15.7 %fusion.31 = (f32[4,4,128]{2,1,0:T(4,128)S(1)}, f32[4,4,128,1536]{3,2,1,0:T(8,128)}) fusion(f32[4,4,128,1536]{3,2,1,0:T(8,128)} %fusion.30), kind=kOutput, calls=%fused_computation.27.clone.1 | output fusion | flops 12584447 | bytes 25174016 | tf_op jit(solution)/shard_map/while/body/eval_jaxpr/sub | solution.py:61
  866.9 8.7 copy.77
  890.8 27.8 %all_to_all.34 = bf16[4096,4,128]{2,1,0:T(4,128)(2,1)S(1)} all-to-all(bf16[4096,4,128]{2,1,0:T(4,128)(2,1)S(1)} %copy.56), channel_id=1, replica_groups=mesh['seq'=16,'head'=2] {'head'}, dimensions={0} | all-to-all | bytes 8388608 | tf_op jit(solution)/shard_map/all_to_all | solution.py:69
  927.5 9.5 %convolution_convert_fusion = bf16[2048,1024]{1,0:T(8,128)(2,1)} fusion(bf16[2048,1024]{0,1:T(8,128)(2,1)} %bitcast.64, bf16[1024,1024]{1,0:T(8,128)(2,1)} %all-gather.5.cloned.1.call-done), kind=kOutput, calls=%fused_computation.21 | convolution fusion | flops 4297064448 | bytes 10485760 | tf_op jit(solution)/shard_map/dot_general | solution.py:72
  (99 shorter events, 277.2 us)
Async XLA Ops:
  6.5 67.5 %all-gather.3.cloned.1.call-start = ((), (), s32[]{:S(2)}) async-start(), calls=%async_computation.2 | async-start | bytes 6684672 | tf_op jit(solution)/shard_map/all_gather | solution.py:37
  7.3 920.2 %all-gather.5.cloned.1.call-start = ((), (), s32[]{:S(2)}) async-start(), calls=%async_computation.3 | async-start | bytes 2228224 | tf_op jit(solution)/shard_map/all_gather | solution.py:71
  250.8 7.1 copy-start
  250.9 8.4 copy-start.2
  258.0 99.0 %collective-permute-start = (bf16[2048,2,4,128]{3,0,2,1:T(8,128)(2,1)}, bf16[2048,2,4,128]{3,0,2,1:T(8,128)(2,1)}, u32[]{:S(2)}, u32[]{:S(2)}) collective-permute-start(bf16[2048,2,4,128]{3,0,2,1:T(8,128)(2,1)} %get-tuple-element.72), channel_id=1, source_target_pairs={{0,2},{2,4},{4,6},{6,8},{8,10},{10,12},{12,14},{14,16},{16,18},{18... | collective-permute-start | bytes 12582920 | tf_op jit(solution)/shard_map/ppermute | solution.py:22
  259.2 100.2 %collective-permute-start.1 = (bf16[2048,2,4,128]{3,0,2,1:T(8,128)(2,1)}, bf16[2048,2,4,128]{3,0,2,1:T(8,128)(2,1)}, u32[]{:S(2)}, u32[]{:S(2)}) collective-permute-start(bf16[2048,2,4,128]{3,0,2,1:T(8,128)(2,1)} %get-tuple-element.73), channel_id=1, source_target_pairs={{2,0},{4,2},{6,4},{8,6},{10,8},{12,10},{14,12},{16,14},{18,16},{20... | collective-permute-start | bytes 12582920 | tf_op jit(solution)/shard_map/ppermute | solution.py:24
  266.5 92.9 %copy-start.1 = (bf16[4096,2,4,128]{3,0,2,1:T(8,128)(2,1)S(1)}, bf16[4096,2,4,128]{3,0,2,1:T(8,128)(2,1)}, u32[]{:S(2)}) copy-start(bf16[4096,2,4,128]{3,0,2,1:T(8,128)(2,1)} %slice.29) | copy-start | bytes 25165828
Sparse Core Ops, SparseCore 0:
  9.6 64.3 all-gather.2
  259.4 78.7 all-gather.4
where the time goes:
time: 947 us; the launch traced here: 944 us
  local copies, waits for them, and re-layouts  322 us (34%)
  blocking collectives  168 us (18%)
  waiting for transfers between devices  156 us (16%)
  matrix products  151 us (16%)
  other arithmetic  132 us (14%)
  between operations  13.5 us (1%)
    gather x16, local copies, waits for them, and re-layouts, attend(): kv_blocks[list_group].reshape(group_blocks, NBR * BLK, 2, per_device, HD)  148 us
    all_to_all x1, blocking collectives, local(): lax.all_to_all(projected, 'head', split_axis=2, concat_axis=0, tiled=True)  141 us
    sub x8, other arithmetic, attend(): expo = jnp.exp(scores - largest)  126 us
    ppermute x1, waiting for transfers between devices, padded_2(): lax.ppermute(tail, axis, [(i, (i + 1) % count) for i in range(count)])  85.6 us
    while x8, local copies, waits for them, and re-layouts  69.5 us
    all_gather x1, waiting for transfers between devices, local(): full_qkv = lax.all_gather(w_qkv, 'seq', axis=0, tiled=True)  66.7 us
    dot_general x8, matrix products, attend(): jnp.einsum('nhqk,nkhd->nqhd', probs, values, preferred_element_type=jnp.f...  66.2 us
    dot_general x8, matrix products, attend(): jnp.einsum('nqhd,nkhd->nhqk', query_group, keys, preferred_element_type=j...  58.4 us
  transfers between devices with their start and end apart: 4, of which 3 were waited for; matrix products, arithmetic and copies ran while one was open for 59% of the time, Pallas kernels for 0%

commit v1 on v0

v1 whole, which is shorter than its diff:
```python
import functools
import math

import jax
import jax.numpy as jnp
from jax import lax
from jax.experimental import pallas as pl
from jax.experimental.pallas import tpu as pltpu
from jax.sharding import PartitionSpec as P

HEADS = 8
HD = 128
BLK = 128
NBR = 12
PB = 16
D = HEADS * HD
PLANE = PB * BLK
TILE = 512
CUTS = (192, 1216, 512, 128)
LARGE = 2.0**100
MIB = 1 << 20
VMEM_LIMIT = 54 * MIB


def project_kernel(x_ref, w_ref, q_ref, k_ref, vt_ref):
    x = x_ref[...]

    def part(start):
        product = jnp.dot(x, w_ref[:, start : start + 512], preferred_element_type=jnp.float32)
        return product.astype(jnp.bfloat16)

    for col in range(0, D, 512):
        q_ref[:, col : col + 512] = part(col)
        k_ref[:, col : col + 512] = part(D + col)
        vt_ref[col : col + 512, :] = part(2 * D + col).T


def project_cost(rows, columns):
    return pl.CostEstimate(
        flops=2 * rows * D * columns, bytes_accessed=2 * rows * (D + columns), transcendentals=0
    )


def project_own(x, w):
    rows = x.shape[0]
    row_spec = pl.BlockSpec((TILE, D), lambda i: (i, 0))
    return pl.pallas_call(
        project_kernel,
        grid=(rows // TILE,),
        in_specs=[row_spec, pl.BlockSpec(memory_space=pltpu.VMEM)],
        out_specs=[row_spec, row_spec, pl.BlockSpec((D, TILE), lambda i: (0, i))],
        out_shape=[
            jax.ShapeDtypeStruct((rows, D), jnp.bfloat16),
            jax.ShapeDtypeStruct((3 * PLANE, D), jnp.bfloat16),
            jax.ShapeDtypeStruct((D, 3 * PLANE), jnp.bfloat16),
        ],
        compiler_params=pltpu.CompilerParams(vmem_limit_bytes=VMEM_LIMIT),
        cost_estimate=project_cost(rows, 3 * D),
        name="project_qkv",
    )(x, w)


def project_halo_kernel(counts, bases, *refs):
    total = sum(counts)
    x_refs, (w_ref, _, _, k_hbm, vt_hbm, k_ref, vt_ref, k_sem, vt_sem) = refs[:total], refs[total:]
    copies = []
    at = 0
    offset = 0
    for i, count in enumerate(counts):
        pieces = [ref[...] for ref in x_refs[at : at + count]]
        at += count
        x = pieces[0] if count == 1 else jnp.concatenate(pieces, axis=0)
        size = x.shape[0]
        rows = pl.ds(offset, size)
        there = pl.ds(bases[i], size)
        offset += size
        for col in range(D, 2 * D, 512):
            part = jnp.dot(x, w_ref[:, col : col + 512], preferred_element_type=jnp.float32)
            k_ref[rows, col - D : col - D + 512] = part.astype(jnp.bfloat16)
        copies.append(pltpu.make_async_copy(k_ref.at[rows, :], k_hbm.at[there, :], k_sem.at[i]))
        copies[-1].start()
        for col in range(2 * D, 3 * D, 512):
            part = jnp.dot(x, w_ref[:, col : col + 512], preferred_element_type=jnp.float32)
            vt_ref[col - 2 * D : col - 2 * D + 512, rows] = part.astype(jnp.bfloat16).T
        copies.append(pltpu.make_async_copy(vt_ref.at[:, rows], vt_hbm.at[:, there], vt_sem.at[i]))
        copies[-1].start()
    for copy in copies:
        copy.wait()


def project_halo(groups, w, k, vt):
    counts = tuple(len(parts) for parts, _ in groups)
    bases = tuple(base for _, base in groups)
    xs = [part for parts, _ in groups for part in parts]
    rows = sum(x.shape[0] for x in xs)
    vmem = pl.BlockSpec(memory_space=pltpu.VMEM)
    hbm = pl.BlockSpec(memory_space=pltpu.HBM)
    return pl.pallas_call(
        functools.partial(project_halo_kernel, counts, bases),
        in_specs=[vmem] * (len(xs) + 1) + [hbm, hbm],
        out_specs=[hbm, hbm],
        out_shape=[
            jax.ShapeDtypeStruct(k.shape, jnp.bfloat16),
            jax.ShapeDtypeStruct(vt.shape, jnp.bfloat16),
        ],
        input_output_aliases={len(xs) + 1: 0, len(xs) + 2: 1},
        scratch_shapes=[
            pltpu.VMEM((rows, D), jnp.bfloat16),
            pltpu.VMEM((D, rows), jnp.bfloat16),
            pltpu.SemaphoreType.DMA((len(groups),)),
            pltpu.SemaphoreType.DMA((len(groups),)),
        ],
        compiler_params=pltpu.CompilerParams(vmem_limit_bytes=40 * MIB),
        cost_estimate=project_cost(rows, 2 * D),
        name="project_kv_halo",
    )(*xs, w, k, vt)


def update_kernel(early_tile, early_ref, rest_ref, w_ref, o_ref):
    def product(x_ref):
        x = x_ref[...]
        for col in range(0, D, 512):
            part = jnp.dot(x, w_ref[:, col : col + 512], preferred_element_type=jnp.float32)
            o_ref[:, col : col + 512] = part.astype(jnp.bfloat16)

    if early_tile is None:
        product(rest_ref)
        return

    @pl.when(pl.program_id(0) == early_tile)
    def _():
        product(early_ref)

    @pl.when(pl.program_id(0) != early_tile)
    def _():
        product(rest_ref)


def project_update(early, rest, w, early_tile):
    rows = rest.shape[0] + (0 if early_tile is None else early.shape[0])
    tiles = rows // TILE
    if early_tile is None:
        rest_map = lambda i: (i, 0)
    else:
        rest_map = lambda i: (jnp.minimum((i + tiles - early_tile - 1) % tiles, tiles - 2), 0)
    return pl.pallas_call(
        functools.partial(update_kernel, early_tile),
        grid=(tiles,),
        in_specs=[
            pl.BlockSpec((TILE, D), lambda i: (0, 0)),
            pl.BlockSpec((TILE, D), rest_map),
            pl.BlockSpec(memory_space=pltpu.VMEM),
        ],
        out_specs=pl.BlockSpec((TILE, D), lambda i: (i, 0)),
        out_shape=jax.ShapeDtypeStruct((rows, D), jnp.bfloat16),
        compiler_params=pltpu.CompilerParams(vmem_limit_bytes=VMEM_LIMIT),
        cost_estimate=project_cost(rows, D),
        name="project_update",
    )(early, rest, w)


def attend_kernel(first, blocks, lists_ref, q_ref, k_ref, vt_ref, o_ref, *scratch):
    s_ref, p_ref, m_ref, i_ref, l_ref = scratch
    factor = math.log2(math.e) / math.sqrt(HD)
    unroll = 4
    per = 4
    part_rows = per * BLK
    parts = NBR // per

    def listed(position):
        return lax.rem(first + position, q_ref.shape[0] // BLK)

    def starts_of(position):
        block = listed(position)
        return [pl.multiple_of(lists_ref[block, j] * BLK, BLK) for j in range(NBR)]

    def diagonal(position):
        q = q_ref[pl.ds(pl.multiple_of(listed(position) * BLK, BLK), BLK), :]
        zero = jnp.zeros((BLK, HD), jnp.bfloat16)
        return jnp.concatenate(
            [
                jnp.concatenate([q[:, :HD], zero], axis=1),
                jnp.concatenate([zero, q[:, HD:]], axis=1),
            ],
            axis=0,
        )

    def score_part(diag, starts, part):
        keys = jnp.concatenate(
            [k_ref[pl.ds(start, BLK), :] for start in starts[part * per : (part + 1) * per]], axis=0
        )
        return lax.dot_general(
            keys, diag, (((1,), (1,)), ((), ())), preferred_element_type=jnp.float32
        )

    def folded(x, reduce):
        return reduce(x.reshape(part_rows // 8, 8, 2 * BLK), axis=0)

    def expo_part(scores, slot, part, largest):
        expo = jnp.exp2((scores - largest) * factor)
        p_ref[slot, part * part_rows : (part + 1) * part_rows, :] = expo.astype(jnp.bfloat16)
        return folded(expo, jnp.sum)

    def value_product(position, slot, starts):
        values = jnp.concatenate([vt_ref[:, pl.ds(start, BLK)] for start in starts], axis=1)
        out = jnp.dot(values, p_ref[slot], preferred_element_type=jnp.float32)
        for h in range(2):
            part = slice(h * HD, (h + 1) * HD)
            mine = out[part, part] * i_ref[slot, :, part]
            rows = pl.ds(pl.multiple_of(position * BLK, BLK), BLK)
            o_ref[rows, part] = mine.T.astype(jnp.bfloat16)

    def first_part(position, slot):
        scores = score_part(diagonal(position), starts_of(position), 0)
        s_ref[slot] = scores
        m_ref[slot] = folded(scores, jnp.max)

    def step(position, slot):
        largest = jnp.max(m_ref[slot], axis=0, keepdims=True)
        previous = jnp.maximum(position - 1, 0)
        diag = diagonal(position)
        starts = starts_of(position)
        total = expo_part(s_ref[slot], slot, 0, largest)
        first_part(jnp.minimum(position + 1, blocks - 1), 1 - slot)
        for part in range(1, parts):
            total = total + expo_part(score_part(diag, starts, part), slot, part, largest)
            if part == 1:
                value_product(previous, 1 - slot, starts_of(previous))
        row_sum = jnp.sum(total, axis=0, keepdims=True)
        i_ref[slot] = 1.0 / row_sum
        l_ref[...] = jnp.maximum(l_ref[...], row_sum)

    @pl.when(pl.program_id(0) == 0)
    def _():
        p_ref[1] = jnp.zeros_like(p_ref[1])
        i_ref[1] = jnp.zeros_like(i_ref[1])

    l_ref[...] = jnp.zeros_like(l_ref)
    first_part(0, 0)

    @pl.loop(0, blocks // unroll)
    def _(index):
        for i in range(unroll):
            step(index * unroll + i, i % 2)

    value_product(blocks - 1, 1, starts_of(blocks - 1))

    @pl.when(jnp.logical_not(jnp.max(l_ref[...]) < LARGE))
    def _():
        @pl.loop(0, blocks)
        def _(position):
            diag = diagonal(position)
            starts = starts_of(position)
            top = None
            for part in range(parts):
                scores = score_part(diag, starts, part)
                s_ref[part] = scores
                some = folded(scores, jnp.max)
                top = some if top is None else jnp.maximum(top, some)
            largest = jnp.max(top, axis=0, keepdims=True)
            total = None
            for part in range(parts):
                some = expo_part(s_ref[part], 1, part, largest)
                total = some if total is None else total + some
            i_ref[1] = 1.0 / jnp.sum(total, axis=0, keepdims=True)
            value_product(position, 1, starts)


def attend(lists, q, k, vt, first, blocks):
    rows = blocks * BLK
    pair = 2 * HD
    keys = NBR * BLK
    return pl.pallas_call(
        functools.partial(attend_kernel, first, blocks),
        grid_spec=pltpu.PrefetchScalarGridSpec(
            num_scalar_prefetch=1,
            grid=(D // pair,),
            in_specs=[
                pl.BlockSpec((q.shape[0], pair), lambda i, lists: (0, i)),
                pl.BlockSpec((3 * PLANE, pair), lambda i, lists: (0, i)),
                pl.BlockSpec((pair, 3 * PLANE), lambda i, lists: (i, 0)),
            ],
            out_specs=pl.BlockSpec((rows, pair), lambda i, lists: (0, i)),
            scratch_shapes=[
                pltpu.VMEM((3, keys // 3, pair), jnp.float32),
                pltpu.VMEM((2, keys, pair), jnp.bfloat16),
                pltpu.VMEM((2, 8, pair), jnp.float32),
                pltpu.VMEM((2, 1, pair), jnp.float32),
                pltpu.VMEM((1, pair), jnp.float32),
            ],
        ),
        out_shape=jax.ShapeDtypeStruct((rows, D), jnp.bfloat16),
        compiler_params=pltpu.CompilerParams(vmem_limit_bytes=VMEM_LIMIT),
        cost_estimate=pl.CostEstimate(
            flops=4 * rows * keys * D, bytes_accessed=32 * MIB, transcendentals=rows * keys * HEADS
        ),
        name="attend",
    )(lists, q, k, vt)


def local(tokens, w_qkv, w_out, neighbours):
    head_count = lax.axis_size("head")
    seq_count = lax.axis_size("seq")
    rows = tokens.shape[0]
    blocks = rows // BLK
    seq = lax.axis_index("seq")
    head = lax.axis_index("head")
    per_plane = PLANE // rows
    side = head // per_plane
    plane = 2 * seq + side
    tie = lax.optimization_barrier

    hops = []
    for s in range(seq_count):
        for h in range(head_count):
            step = 1 if h < per_plane else -1
            hops.append((s * head_count + h, (s + step) % seq_count * head_count + h))

    def forward(x):
        return lax.ppermute(x, ("seq", "head"), hops)

    planes = 2 * seq_count
    lists = lax.dynamic_slice_in_dim(neighbours, head * blocks, blocks, axis=0)
    offset = jnp.mod(lists // PB - plane + 1, planes) - 1
    toward = jnp.where(side == 0, 1, -1)
    slot = jnp.where(offset == 0, 0, jnp.where(offset == toward, 1, 2))
    lists = slot * PB + lists % PB

    w = lax.all_gather(w_qkv, "seq", axis=0, tiled=True)

    if head_count != 2:
        slab = lax.all_gather(tokens, "head", axis=0, tiled=True)
        own = lax.dynamic_slice_in_dim(slab, side * PLANE, PLANE, axis=0)
        other = lax.dynamic_slice_in_dim(slab, (1 - side) * PLANE, PLANE, axis=0)
        far = forward(other)
        q, k, vt = project_own(own, w)
        k, vt = project_halo([([other], PLANE)], w, k, vt)
        k, vt = project_halo([([far], 2 * PLANE)], w, k, vt)
        q = lax.dynamic_slice_in_dim(q, head % per_plane * rows, rows, axis=0)
    else:
        cuts = [0]
        for size in CUTS:
            cuts.append(cuts[-1] + size)

        def swap(x):
            return lax.ppermute(x, "head", [(0, 1), (1, 0)])

        first = tokens[: cuts[1]]
        rest, first = tie((tokens, first))
        x_0 = swap(first)
        later = [rest[start:stop] for start, stop in zip(cuts[1:], cuts[2:])]
        x_0, *later = tie((x_0, *later))
        x_1, x_2, x_3 = [swap(part) for part in later]
        far_0, far_1 = forward(x_0), forward(x_1)
        q, k, vt = project_own(tokens, w)
        x_2, k, vt = tie((x_2, k, vt))
        far_2 = forward(x_2)
        k, vt = project_halo([([x_0, x_1], PLANE)], w, k, vt)
        x_3, k, vt = tie((x_3, k, vt))
        far_3 = forward(x_3)
        k, vt = project_halo(
            [([far_0, far_1], 2 * PLANE), ([x_2, x_3], PLANE + cuts[2])], w, k, vt
        )
        k, vt = project_halo([([far_2, far_3], 2 * PLANE + cuts[2])], w, k, vt)
    k, w_last = tie((k, w_out))
    w_last = lax.all_gather(w_last, "seq", axis=0, tiled=True)
    attended = attend(lists, q, k, vt, 0, blocks)
    return project_update(attended, attended, w_last, None)


def solution(mesh):
    return jax.shard_map(
        local,
        mesh=mesh,
        in_specs=(P(("seq", "head"), None), P("seq", None), P("seq", None), P("seq", None)),
        out_specs=P(("seq", "head"), None),
        check_vma=False,
    )
```

time: 947 us -> 288 us (0.30)
  the two profiles are of different devices: /device:TPU:1 before, /device:TPU:0 now
where the time goes in v1:
time: 288 us; the launch traced here: 287 us
  Pallas kernels  192 us (67%)
  waiting for transfers between devices  65 us (23%)
  between operations  13.5 us (5%)
  starting transfers between devices  8.68 us (3%)
  local copies, waits for them, and re-layouts  7.06 us (2%)
    pallas_call x1, Pallas kernels, attend(): pl.pallas_call(functools.partial(attend_kernel, first, blocks), grid_spec...  140 us
    ppermute x4, waiting for transfers between devices, swap(): return lax.ppermute(x, 'head', [(0, 1), (1, 0)])  62.7 us
    pallas_call x3, Pallas kernels, project_halo(): pl.pallas_call(functools.partial(project_halo_kernel, counts, bases), in_...  25.1 us
    pallas_call x1, Pallas kernels, project_own(): pl.pallas_call(project_kernel, grid=(rows // TILE,), in_specs=[row_spec,...  18.3 us
    pallas_call x1, Pallas kernels, project_update(): pl.pallas_call(functools.partial(update_kernel, early_tile), grid=(tiles,...  8.86 us
    ppermute x4, starting transfers between devices, swap(): return lax.ppermute(x, 'head', [(0, 1), (1, 0)])  8.4 us
    slice x3, local copies, waits for them, and re-layouts, local(): later = [rest[start:stop] for start, stop in zip(cuts[1:], cuts[2:])]  5.87 us
  transfers between devices with their start and end apart: 10, of which 4 were waited for; matrix products, arithmetic and copies ran while one was open for 3% of the time, Pallas kernels for 62%

profile of v1, /device:TPU:0, one launch (start us, length us, event | category | flops | bytes accessed | tf_op | source)
XLA Modules:
  0.0 287.3 jit_solution(2410245748590713423)
XLA Ops:
  6.5 0.7 all-gather.3.cloned.1.call-update
  7.3 0.0 all-gather.5.cloned.1.call-start
  7.3 1.0 slice.12
  8.3 3.0 %collective-permute-start = (bf16[192,1024]{1,0:T(8,128)(2,1)S(1)}, bf16[192,1024]{1,0:T(8,128)(2,1)}, u32[]{:S(2)}, u32[]{:S(2)}) collective-permute-start(bf16[192,1024]{1,0:T(8,128)(2,1)S(1)} %slice.12), channel_id=1, source_target_pairs={{0,1},{1,0},{2,3},{3,2},{4,5},{5,4},{6,7},{7,6},{8,9},{9,8},{10,11... | collective-permute-start | bytes 1179656 | tf_op jit(solution)/shard_map/ppermute | solution.py:346
  11.3 1.9 slice.13
  13.3 2.3 slice.14
  15.6 1.7 slice.15
  17.2 3.3 %collective-permute-done.refs_0_ = bf16[192,1024]{1,0:T(8,128)(2,1)} collective-permute-done((bf16[192,1024]{1,0:T(8,128)(2,1)S(1)}, bf16[192,1024]{1,0:T(8,128)(2,1)}, u32[]{:S(2)}, u32[]{:S(2)}) %collective-permute-start) | collective-permute-done | bytes 393248 | tf_op jit(solution)/shard_map/ppermute | solution.py:346
  20.6 1.7 collective-permute-start.4
  22.3 53.5 %collective-permute-done.4.refs_1_ = bf16[1216,1024]{1,0:T(8,128)(2,1)S(1)} collective-permute-done((bf16[1216,1024]{1,0:T(8,128)(2,1)S(1)}, bf16[1216,1024]{1,0:T(8,128)(2,1)S(1)}, u32[]{:S(2)}, u32[]{:S(2)}) %collective-permute-start.4) | collective-permute-done | bytes 2490400 | tf_op jit(solution)/shard_map/ppermute | solution.py:346
  75.8 0.0 collective-permute-start.7
  75.8 3.6 %collective-permute-start.1 = (bf16[512,1024]{1,0:T(8,128)(2,1)}, bf16[512,1024]{1,0:T(8,128)(2,1)S(1)}, u32[]{:S(2)}, u32[]{:S(2)}) collective-permute-start(bf16[512,1024]{1,0:T(8,128)(2,1)} %slice.14), channel_id=1, source_target_pairs={{0,1},{1,0},{2,3},{3,2},{4,5},{5,4},{6,7},{7,6},{8,9},{9,8},{10,11... | collective-permute-start | bytes 3145736 | tf_op jit(solution)/shard_map/ppermute | solution.py:346
  79.4 0.0 collective-permute-start.3
  79.5 0.0 collective-permute-start.6
  79.5 18.3 %project_qkv.1 = (bf16[2048,1024]{1,0:T(8,128)(2,1)}, bf16[6144,1024]{1,0:T(8,128)(2,1)}, bf16[1024,6144]{1,0:T(8,128)(2,1)}) custom-call(bf16[2048,1024]{1,0:T(8,128)(2,1)} %x_ref.1, bf16[1024,3072]{1,0:T(8,128)(2,1)} %all-gather.3.cloned.1.call-done.w_ref.refs_2_.refs_4_), custom_call_target="tpu_custom_call" | custom-call | flops 12884901888 | bytes 16777216 | tf_op jit(solution)/shard_map/project_qkv/pallas_call | solution.py:47
  97.8 5.9 %collective-permute-done.1.refs_2_ = bf16[512,1024]{1,0:T(8,128)(2,1)S(1)} collective-permute-done((bf16[512,1024]{1,0:T(8,128)(2,1)}, bf16[512,1024]{1,0:T(8,128)(2,1)S(1)}, u32[]{:S(2)}, u32[]{:S(2)}) %collective-permute-start.1) | collective-permute-done | bytes 1048608 | tf_op jit(solution)/shard_map/ppermute | solution.py:346
  103.6 0.0 collective-permute-start.2
  103.7 8.9 %project_kv_halo.3 = (bf16[6144,1024]{1,0:T(8,128)(2,1)}, bf16[1024,6144]{1,0:T(8,128)(2,1)}) custom-call(bf16[192,1024]{1,0:T(8,128)(2,1)} %collective-permute-done.refs_0_, bf16[1216,1024]{1,0:T(8,128)(2,1)S(1)} %collective-permute-done.4.refs_1_, bf16[1024,3072]{1,0:T(8,128)(2,1)S(1)} %copy-done.1, ...), custom_call_target="tpu_custom_call", output_to_operand_aliasing={{0}: (3, {}), {1}: (4, {})} | custom-call | flops 5905580032 | bytes 8650752 | tf_op jit(solution)/shard_map/project_kv_halo/pallas_call | solution.py:98
  112.6 0.0 collective-permute-done.3.refs_3_
  112.6 0.2 collective-permute-start.5
  112.8 0.0 collective-permute-done.6.refs_0_
  112.8 0.0 collective-permute-done.7.refs_1_
  112.8 12.1 %project_kv_halo.4 = (bf16[6144,1024]{1,0:T(8,128)(2,1)}, bf16[1024,6144]{1,0:T(8,128)(2,1)}) custom-call(bf16[192,1024]{1,0:T(8,128)(2,1)} %collective-permute-done.6.refs_0_, bf16[1216,1024]{1,0:T(8,128)(2,1)} %collective-permute-done.7.refs_1_, ...), custom_call_target="tpu_custom_call", output_to_operand_aliasing={{0}: (5, {}), {1}: (6, {})} | custom-call | flops 8589934592 | bytes 12582912 | tf_op jit(solution)/shard_map/project_kv_halo/pallas_call | solution.py:98
  124.9 1.5 collective-permute-done.5.refs_1_
  126.4 0.0 collective-permute-done.2.refs_0_
  126.4 4.1 %project_kv_halo.5 = (bf16[6144,1024]{1,0:T(8,128)(2,1)}, bf16[1024,6144]{1,0:T(8,128)(2,1)}) custom-call(bf16[512,1024]{1,0:T(8,128)(2,1)S(1)} %collective-permute-done.2.refs_0_, bf16[128,1024]{1,0:T(8,128)(2,1)S(1)} %collective-permute-done.5.refs_1_, bf16[1024,3072]{1,0:T(8,128)(2,1)S(1)} %copy-done.1, ...), custom_call_target="tpu_custom_call", output_to_operand_aliasing={{0}: (3, {}), {1}: (4, {})} | custom-call | flops 2684354560 | bytes 3932160 | tf_op jit(solution)/shard_map/project_kv_halo/pallas_call | solution.py:98
  130.6 0.0 all-gather.5.cloned.1.call-update
  130.6 0.1 constant_dynamic-slice_fusion
  130.7 0.1 copy.12
  130.8 0.6 fusion.4.lists_ref
  131.4 140.2 %attend.1.early_ref.rest_ref = bf16[2048,1024]{1,0:T(8,128)(2,1)} custom-call(s32[16,12]{1,0:T(8,128)} %fusion.4.lists_ref, bf16[2048,1024]{1,0:T(8,128)(2,1)} %get-tuple-element.28.q_ref, bf16[6144,1024]{1,0:T(8,128)(2,1)} %get-tuple-element.48.k_ref, bf16[1024,6144]{1,0:T(8,128)(2,1)} %get-tuple-element.49.vt_ref), custom_call_target="tpu_custom_call" | custom-call | flops 12884901888 | bytes 33554432 | tf_op jit(solution)/shard_map/attend/pallas_call | solution.py:273
  271.6 8.9 %project_update.1 = bf16[2048,1024]{1,0:T(8,128)(2,1)} custom-call(bf16[2048,1024]{1,0:T(8,128)(2,1)} %attend.1.early_ref.rest_ref, bf16[2048,1024]{1,0:T(8,128)(2,1)} %attend.1.early_ref.rest_ref, bf16[1024,1024]{1,0:T(8,128)(2,1)} %all-gather.5.cloned.1.call-done.w_ref), custom_call_target="tpu_custom_call" | custom-call | flops 4294967296 | bytes 8388608 | tf_op jit(solution)/shard_map/project_update/pallas_call | solution.py:146
  (7 shorter events, 0.0 us)
Async XLA Ops:
  6.5 124.1 %copy-start = (s32[32,12]{0,1:T(8,128)S(1)}, s32[32,12]{0,1:T(8,128)}, u32[]{:S(2)}) copy-start(s32[32,12]{0,1:T(8,128)} %param.7) | copy-start | bytes 4612
  6.5 72.9 %all-gather.3.cloned.1.call-start = ((), (), s32[]{:S(2)}) async-start(), calls=%async_computation | async-start | bytes 6684672 | tf_op jit(solution)/shard_map/all_gather | solution.py:329
  7.3 264.4 %all-gather.5.cloned.1.call-start = ((), (), s32[]{:S(2)}) async-start(), calls=%async_computation.1 | async-start | bytes 2228224 | tf_op jit(solution)/shard_map/all_gather | solution.py:366
  8.3 12.2 %collective-permute-start = (bf16[192,1024]{1,0:T(8,128)(2,1)S(1)}, bf16[192,1024]{1,0:T(8,128)(2,1)}, u32[]{:S(2)}, u32[]{:S(2)}) collective-permute-start(bf16[192,1024]{1,0:T(8,128)(2,1)S(1)} %slice.12), channel_id=1, source_target_pairs={{0,1},{1,0},{2,3},{3,2},{4,5},{5,4},{6,7},{7,6},{8,9},{9,8},{10,11... | collective-permute-start | bytes 1179656 | tf_op jit(solution)/shard_map/ppermute | solution.py:346
  20.6 55.2 %collective-permute-start.4 = (bf16[1216,1024]{1,0:T(8,128)(2,1)S(1)}, bf16[1216,1024]{1,0:T(8,128)(2,1)S(1)}, u32[]{:S(2)}, u32[]{:S(2)}) collective-permute-start(bf16[1216,1024]{1,0:T(8,128)(2,1)S(1)} %slice.13), channel_id=1, source_target_pairs={{0,1},{1,0},{2,3},{3,2},{4,5},{5,4},{6,7},{7,6},{8,9},{9,8},{10,11... | collective-permute-start | bytes 7471112 | tf_op jit(solution)/shard_map/ppermute | solution.py:346
  75.8 37.0 %collective-permute-start.7 = (bf16[1216,1024]{1,0:T(8,128)(2,1)S(1)}, bf16[1216,1024]{1,0:T(8,128)(2,1)}, u32[]{:S(2)}, u32[]{:S(2)}) collective-permute-start(bf16[1216,1024]{1,0:T(8,128)(2,1)S(1)} %collective-permute-done.4.refs_1_), channel_id=1, source_target_pairs={{0,2},{1,31},{2,4},{3,1},{4,6},{5,3},{6,8},{7,5},{8,10},{9,7},{10,... | collective-permute-start | bytes 7471112 | tf_op jit(solution)/shard_map/ppermute | solution.py:320
  75.8 27.8 %collective-permute-start.1 = (bf16[512,1024]{1,0:T(8,128)(2,1)}, bf16[512,1024]{1,0:T(8,128)(2,1)S(1)}, u32[]{:S(2)}, u32[]{:S(2)}) collective-permute-start(bf16[512,1024]{1,0:T(8,128)(2,1)} %slice.14), channel_id=1, source_target_pairs={{0,1},{1,0},{2,3},{3,2},{4,5},{5,4},{6,7},{7,6},{8,9},{9,8},{10,11... | collective-permute-start | bytes 3145736 | tf_op jit(solution)/shard_map/ppermute | solution.py:346
  79.4 33.1 %collective-permute-start.3 = (bf16[128,1024]{1,0:T(8,128)(2,1)}, bf16[128,1024]{1,0:T(8,128)(2,1)}, u32[]{:S(2)}, u32[]{:S(2)}) collective-permute-start(bf16[128,1024]{1,0:T(8,128)(2,1)} %slice.15), channel_id=1, source_target_pairs={{0,1},{1,0},{2,3},{3,2},{4,5},{5,4},{6,7},{7,6},{8,9},{9,8},{10,11... | collective-permute-start | bytes 786440 | tf_op jit(solution)/shard_map/ppermute | solution.py:346
  79.5 33.4 %collective-permute-start.6 = (bf16[192,1024]{1,0:T(8,128)(2,1)}, bf16[192,1024]{1,0:T(8,128)(2,1)}, u32[]{:S(2)}, u32[]{:S(2)}) collective-permute-start(bf16[192,1024]{1,0:T(8,128)(2,1)} %collective-permute-done.refs_0_), channel_id=1, source_target_pairs={{0,2},{1,31},{2,4},{3,1},{4,6},{5,3},{6,8},{7,5},{8,10},{9,7},{10,... | collective-permute-start | bytes 1179656 | tf_op jit(solution)/shard_map/ppermute | solution.py:320
  79.5 24.2 %copy-start.1 = (bf16[1024,3072]{1,0:T(8,128)(2,1)S(1)}, bf16[1024,3072]{1,0:T(8,128)(2,1)}, u32[]{:S(2)}) copy-start(bf16[1024,3072]{1,0:T(8,128)(2,1)} %all-gather.3.cloned.1.call-done.w_ref.refs_2_.refs_4_) | copy-start | bytes 18874372
  103.6 22.8 %collective-permute-start.2 = (bf16[512,1024]{1,0:T(8,128)(2,1)S(1)}, bf16[512,1024]{1,0:T(8,128)(2,1)S(1)}, u32[]{:S(2)}, u32[]{:S(2)}) collective-permute-start(bf16[512,1024]{1,0:T(8,128)(2,1)S(1)} %collective-permute-done.1.refs_2_), channel_id=1, source_target_pairs={{0,2},{1,31},{2,4},{3,1},{4,6},{5,3},{6,8},{7,5},{8,10},{9,7},{10,... | collective-permute-start | bytes 3145736 | tf_op jit(solution)/shard_map/ppermute | solution.py:320
  112.6 13.9 %collective-permute-start.5 = (bf16[128,1024]{1,0:T(8,128)(2,1)}, bf16[128,1024]{1,0:T(8,128)(2,1)S(1)}, u32[]{:S(2)}, u32[]{:S(2)}) collective-permute-start(bf16[128,1024]{1,0:T(8,128)(2,1)} %collective-permute-done.3.refs_3_), channel_id=1, source_target_pairs={{0,2},{1,31},{2,4},{3,1},{4,6},{5,3},{6,8},{7,5},{8,10},{9,7},{10,... | collective-permute-start | bytes 786440 | tf_op jit(solution)/shard_map/ppermute | solution.py:320
Sparse Core Ops, SparseCore 0:
  9.6 64.5 all-gather.2
  130.7 40.4 all-gather.4

commit v2 on v1

--- a/solution.py
+++ b/solution.py
@@ -16,23 +16,26 @@
 D = HEADS * HD
 PLANE = PB * BLK
 TILE = 512
-CUTS = (192, 1216, 512, 128)
+CUTS = (192, 960, 640, 256)
 LARGE = 2.0**100
 MIB = 1 << 20
 VMEM_LIMIT = 54 * MIB
 
 
-def project_kernel(x_ref, w_ref, q_ref, k_ref, vt_ref):
+def project_kv_kernel(x_ref, w_ref, k_ref, vt_ref):
     x = x_ref[...]
-
-    def part(start):
-        product = jnp.dot(x, w_ref[:, start : start + 512], preferred_element_type=jnp.float32)
-        return product.astype(jnp.bfloat16)
-
     for col in range(0, D, 512):
-        q_ref[:, col : col + 512] = part(col)
-        k_ref[:, col : col + 512] = part(D + col)
-        vt_ref[col : col + 512, :] = part(2 * D + col).T
+        part = jnp.dot(x, w_ref[:, col : col + 512], preferred_element_type=jnp.float32)
+        k_ref[:, col : col + 512] = part.astype(jnp.bfloat16)
+        part = jnp.dot(x, w_ref[:, D + col : D + col + 512], preferred_element_type=jnp.float32)
+        vt_ref[col : col + 512, :] = part.astype(jnp.bfloat16).T
+
+
+def project_q_kernel(x_ref, w_ref, q_ref):
+    x = x_ref[...]
+    for col in range(0, D, 512):
+        part = jnp.dot(x, w_ref[:, col : col + 512], preferred_element_type=jnp.float32)
+        q_ref[:, col : col + 512] = part.astype(jnp.bfloat16)
 
 
 def project_cost(rows, columns):
@@ -41,22 +44,27 @@
     )
 
 
-def project_own(x, w):
+def project_rows(x, w, with_kv):
     rows = x.shape[0]
     row_spec = pl.BlockSpec((TILE, D), lambda i: (i, 0))
+    if with_kv:
+        out_specs = [row_spec, pl.BlockSpec((D, TILE), lambda i: (0, i))]
+        out_shape = [
+            jax.ShapeDtypeStruct((3 * PLANE, D), jnp.bfloat16),
+            jax.ShapeDtypeStruct((D, 3 * PLANE), jnp.bfloat16),
+        ]
+    else:
+        out_specs = row_spec
+        out_shape = jax.ShapeDtypeStruct((rows, D), jnp.bfloat16)
     return pl.pallas_call(
-        project_kernel,
+        project_kv_kernel if with_kv else project_q_kernel,
         grid=(rows // TILE,),
         in_specs=[row_spec, pl.BlockSpec(memory_space=pltpu.VMEM)],
-        out_specs=[row_spec, row_spec, pl.BlockSpec((D, TILE), lambda i: (0, i))],
-        out_shape=[
-            jax.ShapeDtypeStruct((rows, D), jnp.bfloat16),
-            jax.ShapeDtypeStruct((3 * PLANE, D), jnp.bfloat16),
-            jax.ShapeDtypeStruct((D, 3 * PLANE), jnp.bfloat16),
-        ],
+        out_specs=out_specs,
+        out_shape=out_shape,
         compiler_params=pltpu.CompilerParams(vmem_limit_bytes=VMEM_LIMIT),
-        cost_estimate=project_cost(rows, 3 * D),
-        name="project_qkv",
+        cost_estimate=project_cost(rows, w.shape[1]),
+        name="project_kv" if with_kv else "project_q",
     )(x, w)
 
 
@@ -74,14 +82,14 @@
         rows = pl.ds(offset, size)
         there = pl.ds(bases[i], size)
         offset += size
-        for col in range(D, 2 * D, 512):
+        for col in range(0, D, 512):
             part = jnp.dot(x, w_ref[:, col : col + 512], preferred_element_type=jnp.float32)
-            k_ref[rows, col - D : col - D + 512] = part.astype(jnp.bfloat16)
+            k_ref[rows, col : col + 512] = part.astype(jnp.bfloat16)
         copies.append(pltpu.make_async_copy(k_ref.at[rows, :], k_hbm.at[there, :], k_sem.at[i]))
         copies[-1].start()
-        for col in range(2 * D, 3 * D, 512):
-            part = jnp.dot(x, w_ref[:, col : col + 512], preferred_element_type=jnp.float32)
-            vt_ref[col - 2 * D : col - 2 * D + 512, rows] = part.astype(jnp.bfloat16).T
+        for col in range(0, D, 512):
+            part = jnp.dot(x, w_ref[:, D + col : D + col + 512], preferred_element_type=jnp.float32)
+            vt_ref[col : col + 512, rows] = part.astype(jnp.bfloat16).T
         copies.append(pltpu.make_async_copy(vt_ref.at[:, rows], vt_hbm.at[:, there], vt_sem.at[i]))
         copies[-1].start()
     for copy in copies:
@@ -160,12 +168,11 @@
 
 
 def attend_kernel(first, blocks, lists_ref, q_ref, k_ref, vt_ref, o_ref, *scratch):
-    s_ref, p_ref, m_ref, i_ref, l_ref = scratch
+    s_ref, p_ref, m_ref, l_ref = scratch
     factor = math.log2(math.e) / math.sqrt(HD)
     unroll = 4
-    per = 4
-    part_rows = per * BLK
-    parts = NBR // per
+    edges = (0, 2, 7, 12)
+    parts = len(edges) - 1
 
     def listed(position):
         return lax.rem(first + position, q_ref.shape[0] // BLK)
@@ -187,53 +194,53 @@
 
     def score_part(diag, starts, part):
         keys = jnp.concatenate(
-            [k_ref[pl.ds(start, BLK), :] for start in starts[part * per : (part + 1) * per]], axis=0
+            [k_ref[pl.ds(start, BLK), :] for start in starts[edges[part] : edges[part + 1]]], axis=0
         )
         return lax.dot_general(
             keys, diag, (((1,), (1,)), ((), ())), preferred_element_type=jnp.float32
         )
 
-    def folded(x, reduce):
-        return reduce(x.reshape(part_rows // 8, 8, 2 * BLK), axis=0)
+    def folded_max(x):
+        return jnp.max(x.reshape(x.shape[0] // 8, 8, 2 * BLK), axis=0)
 
     def expo_part(scores, slot, part, largest):
         expo = jnp.exp2((scores - largest) * factor)
-        p_ref[slot, part * part_rows : (part + 1) * part_rows, :] = expo.astype(jnp.bfloat16)
-        return folded(expo, jnp.sum)
-
-    def value_product(position, slot, starts):
+        p_ref[slot, edges[part] * BLK : edges[part + 1] * BLK, :] = expo.astype(jnp.bfloat16)
+
+    def value_product(position, slot):
+        starts = starts_of(position)
         values = jnp.concatenate([vt_ref[:, pl.ds(start, BLK)] for start in starts], axis=1)
+        values = jnp.concatenate([values, jnp.ones((16, NBR * BLK), jnp.bfloat16)], axis=0)
         out = jnp.dot(values, p_ref[slot], preferred_element_type=jnp.float32)
+        row_sum = out[2 * HD : 2 * HD + 1, :]
+        inverse = 1.0 / row_sum
         for h in range(2):
             part = slice(h * HD, (h + 1) * HD)
-            mine = out[part, part] * i_ref[slot, :, part]
+            mine = out[part, part] * inverse[:, part]
             rows = pl.ds(pl.multiple_of(position * BLK, BLK), BLK)
             o_ref[rows, part] = mine.T.astype(jnp.bfloat16)
+        return row_sum
 
     def first_part(position, slot):
         scores = score_part(diagonal(position), starts_of(position), 0)
-        s_ref[slot] = scores
-        m_ref[slot] = folded(scores, jnp.max)
+        s_ref[slot, : scores.shape[0], :] = scores
+        m_ref[slot] = folded_max(scores)
 
     def step(position, slot):
         largest = jnp.max(m_ref[slot], axis=0, keepdims=True)
-        previous = jnp.maximum(position - 1, 0)
         diag = diagonal(position)
         starts = starts_of(position)
-        total = expo_part(s_ref[slot], slot, 0, largest)
+        expo_part(s_ref[slot, : edges[1] * BLK, :], slot, 0, largest)
         first_part(jnp.minimum(position + 1, blocks - 1), 1 - slot)
         for part in range(1, parts):
-            total = total + expo_part(score_part(diag, starts, part), slot, part, largest)
+            expo_part(score_part(diag, starts, part), slot, part, largest)
             if part == 1:
-                value_product(previous, 1 - slot, starts_of(previous))
-        row_sum = jnp.sum(total, axis=0, keepdims=True)
-        i_ref[slot] = 1.0 / row_sum
-        l_ref[...] = jnp.maximum(l_ref[...], row_sum)
+                row_sum = value_product(jnp.maximum(position - 1, 0), 1 - slot)
+                l_ref[...] = jnp.maximum(l_ref[...], row_sum)
 
     @pl.when(pl.program_id(0) == 0)
     def _():
-        p_ref[1] = jnp.zeros_like(p_ref[1])
-        i_ref[1] = jnp.zeros_like(i_ref[1])
+        p_ref[1] = jnp.ones_like(p_ref[1])
 
     l_ref[...] = jnp.zeros_like(l_ref)
     first_part(0, 0)
@@ -243,9 +250,10 @@
         for i in range(unroll):
             step(index * unroll + i, i % 2)
 
-    value_product(blocks - 1, 1, starts_of(blocks - 1))
-
-    @pl.when(jnp.logical_not(jnp.max(l_ref[...]) < LARGE))
+    row_sum = value_product(blocks - 1, 1)
+    row_sum = jnp.maximum(l_ref[...], row_sum)
+
+    @pl.when(jnp.logical_not(jnp.max(row_sum) < LARGE))
     def _():
         @pl.loop(0, blocks)
         def _(position):
@@ -254,16 +262,14 @@
             top = None
             for part in range(parts):
                 scores = score_part(diag, starts, part)
-                s_ref[part] = scores
-                some = folded(scores, jnp.max)
+                s_ref[part, : scores.shape[0], :] = scores
+                some = folded_max(scores)
                 top = some if top is None else jnp.maximum(top, some)
             largest = jnp.max(top, axis=0, keepdims=True)
-            total = None
             for part in range(parts):
-                some = expo_part(s_ref[part], 1, part, largest)
-                total = some if total is None else total + some
-            i_ref[1] = 1.0 / jnp.sum(total, axis=0, keepdims=True)
-            value_product(position, 1, starts)
+                size = (edges[part + 1] - edges[part]) * BLK
+                expo_part(s_ref[part, :size, :], 1, part, largest)
+            value_product(position, 1)
 
 
 def attend(lists, q, k, vt, first, blocks):
@@ -282,10 +288,9 @@
             ],
             out_specs=pl.BlockSpec((rows, pair), lambda i, lists: (0, i)),
             scratch_shapes=[
-                pltpu.VMEM((3, keys // 3, pair), jnp.float32),
+                pltpu.VMEM((3, 5 * BLK, pair), jnp.float32),
                 pltpu.VMEM((2, keys, pair), jnp.bfloat16),
                 pltpu.VMEM((2, 8, pair), jnp.float32),
-                pltpu.VMEM((2, 1, pair), jnp.float32),
                 pltpu.VMEM((1, pair), jnp.float32),
             ],
         ),
@@ -326,17 +331,18 @@
     slot = jnp.where(offset == 0, 0, jnp.where(offset == toward, 1, 2))
     lists = slot * PB + lists % PB
 
-    w = lax.all_gather(w_qkv, "seq", axis=0, tiled=True)
+    w_kv = lax.all_gather(w_qkv[:, D:], "seq", axis=0, tiled=True)
+    w_q = lax.all_gather(w_qkv[:, :D], "seq", axis=0, tiled=True)
 
     if head_count != 2:
         slab = lax.all_gather(tokens, "head", axis=0, tiled=True)
         own = lax.dynamic_slice_in_dim(slab, side * PLANE, PLANE, axis=0)
         other = lax.dynamic_slice_in_dim(slab, (1 - side) * PLANE, PLANE, axis=0)
         far = forward(other)
-        q, k, vt = project_own(own, w)
-        k, vt = project_halo([([other], PLANE)], w, k, vt)
-        k, vt = project_halo([([far], 2 * PLANE)], w, k, vt)
-        q = lax.dynamic_slice_in_dim(q, head % per_plane * rows, rows, axis=0)
+        k, vt = project_rows(own, w_kv, True)
+        k, vt = project_halo([([other], PLANE)], w_kv, k, vt)
+        k, vt = project_halo([([far], 2 * PLANE)], w_kv, k, vt)
+        q = project_rows(tokens, w_q, False)
     else:
         cuts = [0]
         for size in CUTS:
@@ -352,16 +358,20 @@
         x_0, *later = tie((x_0, *later))
         x_1, x_2, x_3 = [swap(part) for part in later]
         far_0, far_1 = forward(x_0), forward(x_1)
-        q, k, vt = project_own(tokens, w)
+        k, vt = project_rows(tokens, w_kv, True)
+        x_1, k, vt = tie((x_1, k, vt))
+        k, vt = project_halo([([x_0, x_1], PLANE)], w_kv, k, vt)
+        k, vt = project_halo([([far_0, far_1], 2 * PLANE)], w_kv, k, vt)
         x_2, k, vt = tie((x_2, k, vt))
         far_2 = forward(x_2)
-        k, vt = project_halo([([x_0, x_1], PLANE)], w, k, vt)
+        k, vt = project_halo([([x_2], PLANE + cuts[2])], w_kv, k, vt)
         x_3, k, vt = tie((x_3, k, vt))
         far_3 = forward(x_3)
+        q = project_rows(tokens, w_q, False)
+        k, vt, q = tie((k, vt, q))
         k, vt = project_halo(
-            [([far_0, far_1], 2 * PLANE), ([x_2, x_3], PLANE + cuts[2])], w, k, vt
+            [([x_3], PLANE + cuts[3]), ([far_2, far_3], 2 * PLANE + cuts[2])], w_kv, k, vt
         )
-        k, vt = project_halo([([far_2, far_3], 2 * PLANE + cuts[2])], w, k, vt)
     k, w_last = tie((k, w_out))
     w_last = lax.all_gather(w_last, "seq", axis=0, tiled=True)
     attended = attend(lists, q, k, vt, 0, blocks)

time: 288 us -> 305 us (1.059)
  Pallas kernels: 192 us -> 200 us
  starting transfers between devices: 8.68 us -> 14.7 us
  local copies, waits for them, and re-layouts: 7.06 us -> 11.8 us
    ppermute x4, waiting for transfers between devices: 62.7 us -> 46.5 us  [swap(): return lax.ppermute(x, 'head', [(0, 1), (1, 0)])]
    ppermute x4, waiting for transfers between devices: 1.54 us -> 17.4 us  [forward(): return lax.ppermute(x, ('seq', 'head'), hops)]
    ppermute x4, starting transfers between devices: 8.4 us -> 12.9 us  [swap(): return lax.ppermute(x, 'head', [(0, 1), (1, 0)])]
    pallas_call x1 -> x2, Pallas kernels: 18.3 us -> 21.9 us  [project_rows(): pl.pallas_call(project_kv_kernel if with_kv else project_q_kernel, grid=(...]
    slice x0 -> x2, local copies, waits for them, and re-layouts: none -> 3.24 us  [the longest x1 1.68 us: local(): w_kv = lax.all_gather(w_qkv[:, D:], 'seq', axis=0, tiled=True)]
    pallas_call x3 -> x4, Pallas kernels: 25.1 us -> 27.8 us  [project_halo(): pl.pallas_call(functools.partial(project_halo_kernel, counts, bases), in_...]
  transfers between devices with their start and end apart: 10 -> 11, of which waited for: 4 -> 6; matrix products, arithmetic and copies ran while one was open for 3% -> 4% of each run, Pallas kernels for 62% -> 60%
where the time goes in v2:
time: 305 us
  Pallas kernels  200 us (66%)
  waiting for transfers between devices  64.3 us (21%)
  starting transfers between devices  14.7 us (5%)
  between operations  13.2 us (4%)
  local copies, waits for them, and re-layouts  11.8 us (4%)
    pallas_call x1, Pallas kernels, attend(): pl.pallas_call(functools.partial(attend_kernel, first, blocks), grid_spec...  142 us
    ppermute x4, waiting for transfers between devices, swap(): return lax.ppermute(x, 'head', [(0, 1), (1, 0)])  46.5 us
    pallas_call x4, Pallas kernels, project_halo(): pl.pallas_call(functools.partial(project_halo_kernel, counts, bases), in_...  27.8 us
    pallas_call x2, Pallas kernels, project_rows(): pl.pallas_call(project_kv_kernel if with_kv else project_q_kernel, grid=(...  21.9 us
    ppermute x4, waiting for transfers between devices, forward(): return lax.ppermute(x, ('seq', 'head'), hops)  17.4 us
    ppermute x4, starting transfers between devices, swap(): return lax.ppermute(x, 'head', [(0, 1), (1, 0)])  12.9 us
    pallas_call x1, Pallas kernels, project_update(): pl.pallas_call(functools.partial(update_kernel, early_tile), grid=(tiles,...  8.98 us
    slice x3, local copies, waits for them, and re-layouts, local(): later = [rest[start:stop] for start, stop in zip(cuts[1:], cuts[2:])]  7.33 us
  transfers between devices with their start and end apart: 11, of which 6 were waited for; matrix products, arithmetic and copies ran while one was open for 4% of the time, Pallas kernels for 60%

profile of v2, /device:TPU:0, one launch (start us, length us, event | category | flops | bytes accessed | tf_op | source)
XLA Modules:
  0.0 304.9 jit_solution(9363899256379801861)
XLA Ops:
  6.5 1.7 slice.22
  8.2 0.0 all-gather.6.cloned.1.call-start
  8.3 1.0 slice.18
  9.3 3.0 collective-permute-start
  12.3 3.0 slice.19
  15.3 2.5 slice.20
  17.8 1.9 slice.21
  19.7 1.9 collective-permute-done.refs_0_
  21.5 1.7 collective-permute-start.4
  23.3 1.6 slice.23
  24.9 0.0 all-gather.8.cloned.1.call-start
  24.9 40.8 %collective-permute-done.4.refs_1_ = bf16[960,1024]{1,0:T(8,128)(2,1)S(1)} collective-permute-done((bf16[960,1024]{1,0:T(8,128)(2,1)}, bf16[960,1024]{1,0:T(8,128)(2,1)S(1)}, u32[]{:S(2)}, u32[]{:S(2)}) %collective-permute-start.4) | collective-permute-done | bytes 1966112 | tf_op jit(solution)/shard_map/ppermute | solution.py:352
  65.8 1.6 collective-permute-start.3
  67.3 4.5 %collective-permute-start.2 = (bf16[640,1024]{1,0:T(8,128)(2,1)}, bf16[640,1024]{1,0:T(8,128)(2,1)S(1)}, u32[]{:S(2)}, u32[]{:S(2)}) collective-permute-start(bf16[640,1024]{1,0:T(8,128)(2,1)} %slice.20), channel_id=1, source_target_pairs={{0,1},{1,0},{2,3},{3,2},{4,5},{5,4},{6,7},{7,6},{8,9},{9,8},{10,11... | collective-permute-start | bytes 3932168 | tf_op jit(solution)/shard_map/ppermute | solution.py:352
  71.9 13.4 %project_kv.1 = (bf16[6144,1024]{1,0:T(8,128)(2,1)}, bf16[1024,6144]{1,0:T(8,128)(2,1)}) custom-call(bf16[2048,1024]{1,0:T(8,128)(2,1)} %x_ref.3, bf16[1024,2048]{1,0:T(8,128)(2,1)} %all-gather.4.cloned.1.call-done.w_ref.refs_2_.refs_1_.refs_3_), custom_call_target="tpu_custom_call" | custom-call | flops 8589934592 | bytes 12582912 | tf_op jit(solution)/shard_map/project_kv/pallas_call | solution.py:59
  85.2 7.6 %project_kv_halo.4 = (bf16[6144,1024]{1,0:T(8,128)(2,1)}, bf16[1024,6144]{1,0:T(8,128)(2,1)}) custom-call(bf16[192,1024]{1,0:T(8,128)(2,1)} %collective-permute-done.refs_0_, bf16[960,1024]{1,0:T(8,128)(2,1)S(1)} %collective-permute-done.4.refs_1_, bf16[1024,2048]{1,0:T(8,128)(2,1)S(1)} %copy-done.1, ...), custom_call_target="tpu_custom_call", output_to_operand_aliasing={{0}: (3, {}), {1}: (4, {})} | custom-call | flops 4831838208 | bytes 7077888 | tf_op jit(solution)/shard_map/project_kv_halo/pallas_call | solution.py:106
  92.9 8.2 %collective-permute-done.3.refs_0_ = bf16[192,1024]{1,0:T(8,128)(2,1)} collective-permute-done((bf16[192,1024]{1,0:T(8,128)(2,1)}, bf16[192,1024]{1,0:T(8,128)(2,1)}, u32[]{:S(2)}, u32[]{:S(2)}) %collective-permute-start.3) | collective-permute-done | bytes 393248 | tf_op jit(solution)/shard_map/ppermute | solution.py:325
  101.1 8.4 %project_kv_halo.5 = (bf16[6144,1024]{1,0:T(8,128)(2,1)}, bf16[1024,6144]{1,0:T(8,128)(2,1)}) custom-call(bf16[192,1024]{1,0:T(8,128)(2,1)} %collective-permute-done.3.refs_0_, bf16[960,1024]{1,0:T(8,128)(2,1)} %collective-permute-done.5.refs_1_, bf16[1024,2048]{1,0:T(8,128)(2,1)S(1)} %copy-done.1, ...), custom_call_target="tpu_custom_call", output_to_operand_aliasing={{0}: (3, {}), {1}: (4, {})} | custom-call | flops 4831838208 | bytes 7077888 | tf_op jit(solution)/shard_map/project_kv_halo/pallas_call | solution.py:106
  109.5 0.2 collective-permute-start.6
  109.7 3.6 %collective-permute-start.1 = (bf16[256,1024]{1,0:T(8,128)(2,1)S(1)}, bf16[256,1024]{1,0:T(8,128)(2,1)S(1)}, u32[]{:S(2)}, u32[]{:S(2)}) collective-permute-start(bf16[256,1024]{1,0:T(8,128)(2,1)S(1)} %copy-done.3), channel_id=1, source_target_pairs={{0,1},{1,0},{2,3},{3,2},{4,5},{5,4},{6,7},{7,6},{8,9},{9,8},{10,11... | collective-permute-start | bytes 1572872 | tf_op jit(solution)/shard_map/ppermute | solution.py:352
  113.3 4.2 %project_kv_halo.6 = (bf16[6144,1024]{1,0:T(8,128)(2,1)}, bf16[1024,6144]{1,0:T(8,128)(2,1)}) custom-call(bf16[640,1024]{1,0:T(8,128)(2,1)S(1)} %collective-permute-done.2.refs_0_, bf16[1024,2048]{1,0:T(8,128)(2,1)S(1)} %copy-done.1, bf16[6144,1024]{1,0:T(8,128)(2,1)} %get-tuple-element.51.refs_2_, ...), custom_call_target="tpu_custom_call", output_to_operand_aliasing={{0}: (2, {}), {1}: (3, {})} | custom-call | flops 2684354560 | bytes 3932160 | tf_op jit(solution)/shard_map/project_kv_halo/pallas_call | solution.py:106
  117.5 3.8 %collective-permute-done.1.refs_0_ = bf16[256,1024]{1,0:T(8,128)(2,1)S(1)} collective-permute-done((bf16[256,1024]{1,0:T(8,128)(2,1)S(1)}, bf16[256,1024]{1,0:T(8,128)(2,1)S(1)}, u32[]{:S(2)}, u32[]{:S(2)}) %collective-permute-start.1) | collective-permute-done | bytes 524320 | tf_op jit(solution)/shard_map/ppermute | solution.py:352
  121.3 0.4 all-gather.6.cloned.1.call-done.w_ref
  121.7 8.5 %project_q.1.q_ref = bf16[2048,1024]{1,0:T(8,128)(2,1)} custom-call(bf16[2048,1024]{1,0:T(8,128)(2,1)} %x_ref.3, bf16[1024,1024]{1,0:T(8,128)(2,1)} %all-gather.6.cloned.1.call-done.w_ref), custom_call_target="tpu_custom_call" | custom-call | flops 4294967296 | bytes 8388608 | tf_op jit(solution)/shard_map/project_q/pallas_call | solution.py:59
  130.2 9.2 %collective-permute-done.7.refs_2_ = bf16[256,1024]{1,0:T(8,128)(2,1)} collective-permute-done((bf16[256,1024]{1,0:T(8,128)(2,1)S(1)}, bf16[256,1024]{1,0:T(8,128)(2,1)}, u32[]{:S(2)}, u32[]{:S(2)}) %collective-permute-start.7) | collective-permute-done | bytes 524320 | tf_op jit(solution)/shard_map/ppermute | solution.py:325
  139.4 7.6 %project_kv_halo.7 = (bf16[6144,1024]{1,0:T(8,128)(2,1)}, bf16[1024,6144]{1,0:T(8,128)(2,1)}) custom-call(bf16[256,1024]{1,0:T(8,128)(2,1)S(1)} %collective-permute-done.1.refs_0_, bf16[640,1024]{1,0:T(8,128)(2,1)S(1)} %collective-permute-done.6.refs_1_, ...), custom_call_target="tpu_custom_call", output_to_operand_aliasing={{0}: (4, {}), {1}: (5, {})} | custom-call | flops 4831838208 | bytes 7077888 | tf_op jit(solution)/shard_map/project_kv_halo/pallas_call | solution.py:106
  147.0 0.0 all-gather.8.cloned.1.call-update
  147.0 0.1 constant_dynamic-slice_fusion
  147.1 0.1 copy.14
  147.2 0.6 fusion.4.lists_ref
  147.8 141.5 %attend.1.early_ref.rest_ref = bf16[2048,1024]{1,0:T(8,128)(2,1)} custom-call(s32[16,12]{1,0:T(8,128)} %fusion.4.lists_ref, bf16[2048,1024]{1,0:T(8,128)(2,1)} %project_q.1.q_ref, bf16[6144,1024]{1,0:T(8,128)(2,1)} %get-tuple-element.62.k_ref, bf16[1024,6144]{1,0:T(8,128)(2,1)} %get-tuple-element.63.vt_ref), custom_call_target="tpu_custom_call" | custom-call | flops 12884901888 | bytes 33554432 | tf_op jit(solution)/shard_map/attend/pallas_call | solution.py:279
  289.4 9.0 %project_update.1 = bf16[2048,1024]{1,0:T(8,128)(2,1)} custom-call(bf16[2048,1024]{1,0:T(8,128)(2,1)} %attend.1.early_ref.rest_ref, bf16[2048,1024]{1,0:T(8,128)(2,1)} %attend.1.early_ref.rest_ref, bf16[1024,1024]{1,0:T(8,128)(2,1)} %all-gather.8.cloned.1.call-done.w_ref), custom_call_target="tpu_custom_call" | custom-call | flops 4294967296 | bytes 8388608 | tf_op jit(solution)/shard_map/project_update/pallas_call | solution.py:154
  (18 shorter events, 0.1 us)
Async XLA Ops:
  6.5 140.5 %copy-start = (s32[32,12]{0,1:T(8,128)S(1)}, s32[32,12]{0,1:T(8,128)}, u32[]{:S(2)}) copy-start(s32[32,12]{0,1:T(8,128)} %param.7) | copy-start | bytes 4612
  6.5 65.3 %all-gather.4.cloned.1.call-start = ((), (), s32[]{:S(2)}) async-start(), calls=%async_computation | async-start | bytes 4456448 | tf_op jit(solution)/shard_map/all_gather | solution.py:334
  8.2 113.5 %all-gather.6.cloned.1.call-start = ((), (), s32[]{:S(2)}) async-start(), calls=%async_computation.1 | async-start | bytes 2228224 | tf_op jit(solution)/shard_map/all_gather | solution.py:335
  9.3 12.2 %collective-permute-start = (bf16[192,1024]{1,0:T(8,128)(2,1)S(1)}, bf16[192,1024]{1,0:T(8,128)(2,1)}, u32[]{:S(2)}, u32[]{:S(2)}) collective-permute-start(bf16[192,1024]{1,0:T(8,128)(2,1)S(1)} %slice.18), channel_id=1, source_target_pairs={{0,1},{1,0},{2,3},{3,2},{4,5},{5,4},{6,7},{7,6},{8,9},{9,8},{10,11... | collective-permute-start | bytes 1179656 | tf_op jit(solution)/shard_map/ppermute | solution.py:352
  21.5 44.2 %collective-permute-start.4 = (bf16[960,1024]{1,0:T(8,128)(2,1)}, bf16[960,1024]{1,0:T(8,128)(2,1)S(1)}, u32[]{:S(2)}, u32[]{:S(2)}) collective-permute-start(bf16[960,1024]{1,0:T(8,128)(2,1)} %slice.19), channel_id=1, source_target_pairs={{0,1},{1,0},{2,3},{3,2},{4,5},{5,4},{6,7},{7,6},{8,9},{9,8},{10,11... | collective-permute-start | bytes 5898248 | tf_op jit(solution)/shard_map/ppermute | solution.py:352
  24.9 264.5 %all-gather.8.cloned.1.call-start = ((), (), s32[]{:S(2)}) async-start(), calls=%async_computation.2 | async-start | bytes 2228224 | tf_op jit(solution)/shard_map/all_gather | solution.py:376
  65.8 35.3 %collective-permute-start.5 = (bf16[960,1024]{1,0:T(8,128)(2,1)S(1)}, bf16[960,1024]{1,0:T(8,128)(2,1)}, u32[]{:S(2)}, u32[]{:S(2)}) collective-permute-start(bf16[960,1024]{1,0:T(8,128)(2,1)S(1)} %collective-permute-done.4.refs_1_), channel_id=1, source_target_pairs={{0,2},{1,31},{2,4},{3,1},{4,6},{5,3},{6,8},{7,5},{8,10},{9,7},{10,... | collective-permute-start | bytes 5898248 | tf_op jit(solution)/shard_map/ppermute | solution.py:325
  65.8 35.3 %collective-permute-start.3 = (bf16[192,1024]{1,0:T(8,128)(2,1)}, bf16[192,1024]{1,0:T(8,128)(2,1)}, u32[]{:S(2)}, u32[]{:S(2)}) collective-permute-start(bf16[192,1024]{1,0:T(8,128)(2,1)} %collective-permute-done.refs_0_), channel_id=1, source_target_pairs={{0,2},{1,31},{2,4},{3,1},{4,6},{5,3},{6,8},{7,5},{8,10},{9,7},{10,... | collective-permute-start | bytes 1179656 | tf_op jit(solution)/shard_map/ppermute | solution.py:325
  67.3 42.1 %collective-permute-start.2 = (bf16[640,1024]{1,0:T(8,128)(2,1)}, bf16[640,1024]{1,0:T(8,128)(2,1)S(1)}, u32[]{:S(2)}, u32[]{:S(2)}) collective-permute-start(bf16[640,1024]{1,0:T(8,128)(2,1)} %slice.20), channel_id=1, source_target_pairs={{0,1},{1,0},{2,3},{3,2},{4,5},{5,4},{6,7},{7,6},{8,9},{9,8},{10,11... | collective-permute-start | bytes 3932168 | tf_op jit(solution)/shard_map/ppermute | solution.py:352
  71.9 13.4 %copy-start.1 = (bf16[1024,2048]{1,0:T(8,128)(2,1)S(1)}, bf16[1024,2048]{1,0:T(8,128)(2,1)}, u32[]{:S(2)}) copy-start(bf16[1024,2048]{1,0:T(8,128)(2,1)} %all-gather.4.cloned.1.call-done.w_ref.refs_2_.refs_1_.refs_3_) | copy-start | bytes 12582916
  101.1 8.7 %copy-start.3 = (bf16[256,1024]{1,0:T(8,128)(2,1)S(1)}, bf16[256,1024]{1,0:T(8,128)(2,1)}, u32[]{:S(2)}) copy-start(bf16[256,1024]{1,0:T(8,128)(2,1)} %slice.21) | copy-start | bytes 1572868
  109.5 29.9 %collective-permute-start.6 = (bf16[640,1024]{1,0:T(8,128)(2,1)S(1)}, bf16[640,1024]{1,0:T(8,128)(2,1)S(1)}, u32[]{:S(2)}, u32[]{:S(2)}) collective-permute-start(bf16[640,1024]{1,0:T(8,128)(2,1)S(1)} %collective-permute-done.2.refs_0_), channel_id=1, source_target_pairs={{0,2},{1,31},{2,4},{3,1},{4,6},{5,3},{6,8},{7,5},{8,10},{9,7},{10,... | collective-permute-start | bytes 3932168 | tf_op jit(solution)/shard_map/ppermute | solution.py:325
  109.7 11.6 %collective-permute-start.1 = (bf16[256,1024]{1,0:T(8,128)(2,1)S(1)}, bf16[256,1024]{1,0:T(8,128)(2,1)S(1)}, u32[]{:S(2)}, u32[]{:S(2)}) collective-permute-start(bf16[256,1024]{1,0:T(8,128)(2,1)S(1)} %copy-done.3), channel_id=1, source_target_pairs={{0,1},{1,0},{2,3},{3,2},{4,5},{5,4},{6,7},{7,6},{8,9},{9,8},{10,11... | collective-permute-start | bytes 1572872 | tf_op jit(solution)/shard_map/ppermute | solution.py:352
  121.3 18.1 %collective-permute-start.7 = (bf16[256,1024]{1,0:T(8,128)(2,1)S(1)}, bf16[256,1024]{1,0:T(8,128)(2,1)}, u32[]{:S(2)}, u32[]{:S(2)}) collective-permute-start(bf16[256,1024]{1,0:T(8,128)(2,1)S(1)} %collective-permute-done.1.refs_0_), channel_id=1, source_target_pairs={{0,2},{1,31},{2,4},{3,1},{4,6},{5,3},{6,8},{7,5},{8,10},{9,7},{10,... | collective-permute-start | bytes 1572872 | tf_op jit(solution)/shard_map/ppermute | solution.py:325
  121.7 17.7 %copy-start.2 = (bf16[1024,2048]{1,0:T(8,128)(2,1)S(1)}, bf16[1024,2048]{1,0:T(8,128)(2,1)}, u32[]{:S(2)}) copy-start(bf16[1024,2048]{1,0:T(8,128)(2,1)} %all-gather.4.cloned.1.call-done.w_ref.refs_2_.refs_1_.refs_3_) | copy-start | bytes 12582916
Sparse Core Ops, SparseCore 0:
  9.5 53.2 all-gather.3
  65.0 56.7 all-gather.5
  147.1 39.9 all-gather.7

commit v3 on v2

--- a/solution.py
+++ b/solution.py
@@ -16,26 +16,24 @@
 D = HEADS * HD
 PLANE = PB * BLK
 TILE = 512
-CUTS = (192, 960, 640, 256)
+UPDATE_TILE = 256
+CUTS = (192, 1088, 512, 256)
 LARGE = 2.0**100
 MIB = 1 << 20
 VMEM_LIMIT = 54 * MIB
 
 
-def project_kv_kernel(x_ref, w_ref, k_ref, vt_ref):
+def project_own_kernel(x_ref, w_ref, q_ref, k_ref, vt_ref):
     x = x_ref[...]
+
+    def part(start):
+        product = jnp.dot(x, w_ref[:, start : start + 512], preferred_element_type=jnp.float32)
+        return product.astype(jnp.bfloat16)
+
     for col in range(0, D, 512):
-        part = jnp.dot(x, w_ref[:, col : col + 512], preferred_element_type=jnp.float32)
-        k_ref[:, col : col + 512] = part.astype(jnp.bfloat16)
-        part = jnp.dot(x, w_ref[:, D + col : D + col + 512], preferred_element_type=jnp.float32)
-        vt_ref[col : col + 512, :] = part.astype(jnp.bfloat16).T
-
-
-def project_q_kernel(x_ref, w_ref, q_ref):
-    x = x_ref[...]
-    for col in range(0, D, 512):
-        part = jnp.dot(x, w_ref[:, col : col + 512], preferred_element_type=jnp.float32)
-        q_ref[:, col : col + 512] = part.astype(jnp.bfloat16)
+        q_ref[:, col : col + 512] = part(col)
+        k_ref[:, col : col + 512] = part(D + col)
+        vt_ref[col : col + 512, :] = part(2 * D + col).T
 
 
 def project_cost(rows, columns):
@@ -44,27 +42,21 @@
     )
 
 
-def project_rows(x, w, with_kv):
-    rows = x.shape[0]
+def project_own(x, w):
     row_spec = pl.BlockSpec((TILE, D), lambda i: (i, 0))
-    if with_kv:
-        out_specs = [row_spec, pl.BlockSpec((D, TILE), lambda i: (0, i))]
-        out_shape = [
+    return pl.pallas_call(
+        project_own_kernel,
+        grid=(PLANE // TILE,),
+        in_specs=[row_spec, pl.BlockSpec(memory_space=pltpu.VMEM)],
+        out_specs=[row_spec, row_spec, pl.BlockSpec((D, TILE), lambda i: (0, i))],
+        out_shape=[
+            jax.ShapeDtypeStruct((PLANE, D), jnp.bfloat16),
             jax.ShapeDtypeStruct((3 * PLANE, D), jnp.bfloat16),
             jax.ShapeDtypeStruct((D, 3 * PLANE), jnp.bfloat16),
-        ]
-    else:
-        out_specs = row_spec
-        out_shape = jax.ShapeDtypeStruct((rows, D), jnp.bfloat16)
-    return pl.pallas_call(
-        project_kv_kernel if with_kv else project_q_kernel,
-        grid=(rows // TILE,),
-        in_specs=[row_spec, pl.BlockSpec(memory_space=pltpu.VMEM)],
-        out_specs=out_specs,
-        out_shape=out_shape,
+        ],
         compiler_params=pltpu.CompilerParams(vmem_limit_bytes=VMEM_LIMIT),
-        cost_estimate=project_cost(rows, w.shape[1]),
-        name="project_kv" if with_kv else "project_q",
+        cost_estimate=project_cost(PLANE, 3 * D),
+        name="project_qkv",
     )(x, w)
 
 
@@ -83,12 +75,16 @@
         there = pl.ds(bases[i], size)
         offset += size
         for col in range(0, D, 512):
-            part = jnp.dot(x, w_ref[:, col : col + 512], preferred_element_type=jnp.float32)
+            part = jnp.dot(
+                x, w_ref[:, D + col : D + col + 512], preferred_element_type=jnp.float32
+            )
             k_ref[rows, col : col + 512] = part.astype(jnp.bfloat16)
         copies.append(pltpu.make_async_copy(k_ref.at[rows, :], k_hbm.at[there, :], k_sem.at[i]))
         copies[-1].start()
         for col in range(0, D, 512):
-            part = jnp.dot(x, w_ref[:, D + col : D + col + 512], preferred_element_type=jnp.float32)
+            part = jnp.dot(
+                x, w_ref[:, 2 * D + col : 2 * D + col + 512], preferred_element_type=jnp.float32
+            )
             vt_ref[col : col + 512, rows] = part.astype(jnp.bfloat16).T
         copies.append(pltpu.make_async_copy(vt_ref.at[:, rows], vt_hbm.at[:, there], vt_sem.at[i]))
         copies[-1].start()
@@ -124,47 +120,26 @@
     )(*xs, w, k, vt)
 
 
-def update_kernel(early_tile, early_ref, rest_ref, w_ref, o_ref):
-    def product(x_ref):
-        x = x_ref[...]
-        for col in range(0, D, 512):
-            part = jnp.dot(x, w_ref[:, col : col + 512], preferred_element_type=jnp.float32)
-            o_ref[:, col : col + 512] = part.astype(jnp.bfloat16)
-
-    if early_tile is None:
-        product(rest_ref)
-        return
-
-    @pl.when(pl.program_id(0) == early_tile)
-    def _():
-        product(early_ref)
-
-    @pl.when(pl.program_id(0) != early_tile)
-    def _():
-        product(rest_ref)
-
-
-def project_update(early, rest, w, early_tile):
-    rows = rest.shape[0] + (0 if early_tile is None else early.shape[0])
-    tiles = rows // TILE
-    if early_tile is None:
-        rest_map = lambda i: (i, 0)
-    else:
-        rest_map = lambda i: (jnp.minimum((i + tiles - early_tile - 1) % tiles, tiles - 2), 0)
+def update_kernel(x_ref, w_ref, o_ref):
+    part = jnp.dot(x_ref[...], w_ref[...], preferred_element_type=jnp.float32)
+    o_ref[...] = part.astype(jnp.bfloat16)
+
+
+def project_update(x, w):
+    rows = x.shape[0]
     return pl.pallas_call(
-        functools.partial(update_kernel, early_tile),
-        grid=(tiles,),
+        update_kernel,
+        grid=(rows // UPDATE_TILE,),
         in_specs=[
-            pl.BlockSpec((TILE, D), lambda i: (0, 0)),
-            pl.BlockSpec((TILE, D), rest_map),
-            pl.BlockSpec(memory_space=pltpu.VMEM),
+            pl.BlockSpec((UPDATE_TILE, D), lambda i: (i, 0)),
+            pl.BlockSpec((D, D), lambda i: (0, 0), pipeline_mode=pl.Buffered(1)),
         ],
-        out_specs=pl.BlockSpec((TILE, D), lambda i: (i, 0)),
+        out_specs=pl.BlockSpec((UPDATE_TILE, D), lambda i: (i, 0)),
         out_shape=jax.ShapeDtypeStruct((rows, D), jnp.bfloat16),
         compiler_params=pltpu.CompilerParams(vmem_limit_bytes=VMEM_LIMIT),
         cost_estimate=project_cost(rows, D),
         name="project_update",
-    )(early, rest, w)
+    )(x, w)
 
 
 def attend_kernel(first, blocks, lists_ref, q_ref, k_ref, vt_ref, o_ref, *scratch):
@@ -331,18 +306,17 @@
     slot = jnp.where(offset == 0, 0, jnp.where(offset == toward, 1, 2))
     lists = slot * PB + lists % PB
 
-    w_kv = lax.all_gather(w_qkv[:, D:], "seq", axis=0, tiled=True)
-    w_q = lax.all_gather(w_qkv[:, :D], "seq", axis=0, tiled=True)
+    w = lax.all_gather(w_qkv, "seq", axis=0, tiled=True)
 
     if head_count != 2:
         slab = lax.all_gather(tokens, "head", axis=0, tiled=True)
         own = lax.dynamic_slice_in_dim(slab, side * PLANE, PLANE, axis=0)
         other = lax.dynamic_slice_in_dim(slab, (1 - side) * PLANE, PLANE, axis=0)
         far = forward(other)
-        k, vt = project_rows(own, w_kv, True)
-        k, vt = project_halo([([other], PLANE)], w_kv, k, vt)
-        k, vt = project_halo([([far], 2 * PLANE)], w_kv, k, vt)
-        q = project_rows(tokens, w_q, False)
+        q, k, vt = project_own(own, w)
+        k, vt = project_halo([([other], PLANE)], w, k, vt)
+        k, vt = project_halo([([far], 2 * PLANE)], w, k, vt)
+        q = lax.dynamic_slice_in_dim(q, head % per_plane * rows, rows, axis=0)
     else:
         cuts = [0]
         for size in CUTS:
@@ -358,24 +332,19 @@
         x_0, *later = tie((x_0, *later))
         x_1, x_2, x_3 = [swap(part) for part in later]
         far_0, far_1 = forward(x_0), forward(x_1)
-        k, vt = project_rows(tokens, w_kv, True)
-        x_1, k, vt = tie((x_1, k, vt))
-        k, vt = project_halo([([x_0, x_1], PLANE)], w_kv, k, vt)
-        k, vt = project_halo([([far_0, far_1], 2 * PLANE)], w_kv, k, vt)
+        q, k, vt = project_own(tokens, w)
         x_2, k, vt = tie((x_2, k, vt))
         far_2 = forward(x_2)
-        k, vt = project_halo([([x_2], PLANE + cuts[2])], w_kv, k, vt)
+        k, vt = project_halo([([x_0, x_1], PLANE)], w, k, vt)
         x_3, k, vt = tie((x_3, k, vt))
         far_3 = forward(x_3)
-        q = project_rows(tokens, w_q, False)
-        k, vt, q = tie((k, vt, q))
-        k, vt = project_halo(
-            [([x_3], PLANE + cuts[3]), ([far_2, far_3], 2 * PLANE + cuts[2])], w_kv, k, vt
-        )
+        k, vt = project_halo([([far_0, far_1], 2 * PLANE)], w, k, vt)
+        k, vt = project_halo([([x_2, x_3], PLANE + cuts[2])], w, k, vt)
+        k, vt = project_halo([([far_2, far_3], 2 * PLANE + cuts[2])], w, k, vt)
     k, w_last = tie((k, w_out))
     w_last = lax.all_gather(w_last, "seq", axis=0, tiled=True)
     attended = attend(lists, q, k, vt, 0, blocks)
-    return project_update(attended, attended, w_last, None)
+    return project_update(attended, w_last)
 
 
 def solution(mesh):

time: 305 us -> 290 us (0.951)
  starting transfers between devices: 14.7 us -> 8.55 us
  waiting for transfers between devices: 64.3 us -> 59.3 us
  local copies, waits for them, and re-layouts: 11.8 us -> 7.17 us
    ppermute x4, waiting for transfers between devices: 17.4 us -> 0.01 us  [forward(): return lax.ppermute(x, ('seq', 'head'), hops)]
    ppermute x4, waiting for transfers between devices: 46.5 us -> 56.5 us  [swap(): return lax.ppermute(x, 'head', [(0, 1), (1, 0)])]
    ppermute x4, starting transfers between devices: 12.9 us -> 8.5 us  [swap(): return lax.ppermute(x, 'head', [(0, 1), (1, 0)])]
    slice x2 -> x0, local copies, waits for them, and re-layouts: 3.24 us -> none  [the longest x1 1.68 us: local(): w_kv = lax.all_gather(w_qkv[:, D:], 'seq', axis=0, tiled=True)]
    pallas_call x3 -> x2, Pallas kernels: 30.8 us -> 28.3 us  [the longest x1 18.3 us: project_own(): pl.pallas_call(project_own_kernel, grid=(PLANE // TILE,), in_specs=[row_s...]
  transfers between devices with their start and end apart: 11 -> 10, of which waited for: 6 -> 5; matrix products, arithmetic and copies ran while one was open for 4% -> 3% of each run, Pallas kernels for 60% -> 64%
where the time goes in v3:
time: 290 us; the launch traced here: 288 us
  Pallas kernels  199 us (69%)
  waiting for transfers between devices  59.3 us (20%)
  between operations  13.5 us (5%)
  starting transfers between devices  8.55 us (3%)
  local copies, waits for them, and re-layouts  7.17 us (2%)
    pallas_call x1, Pallas kernels, attend(): pl.pallas_call(functools.partial(attend_kernel, first, blocks), grid_spec...  142 us
    ppermute x4, waiting for transfers between devices, swap(): return lax.ppermute(x, 'head', [(0, 1), (1, 0)])  56.5 us
    pallas_call x4, Pallas kernels, project_halo(): pl.pallas_call(functools.partial(project_halo_kernel, counts, bases), in_...  28.5 us
    pallas_call x1, Pallas kernels, project_own(): pl.pallas_call(project_own_kernel, grid=(PLANE // TILE,), in_specs=[row_s...  18.3 us
    pallas_call x1, Pallas kernels, project_update(): pl.pallas_call(update_kernel, grid=(rows // UPDATE_TILE,), in_specs=[pl.B...  9.98 us
    ppermute x4, starting transfers between devices, swap(): return lax.ppermute(x, 'head', [(0, 1), (1, 0)])  8.5 us
    slice x3, local copies, waits for them, and re-layouts, local(): later = [rest[start:stop] for start, stop in zip(cuts[1:], cuts[2:])]  5.98 us
  transfers between devices with their start and end apart: 10, of which 5 were waited for; matrix products, arithmetic and copies ran while one was open for 3% of the time, Pallas kernels for 64%

profile of v3, /device:TPU:0, one launch (start us, length us, event | category | flops | bytes accessed | tf_op | source)
XLA Modules:
  0.0 287.7 jit_solution(14374681649001956025)
XLA Ops:
  6.5 0.7 all-gather.3.cloned.1.call-update
  7.3 0.0 all-gather.5.cloned.1.call-start
  7.3 1.0 slice.12
  8.3 3.0 %collective-permute-start = (bf16[192,1024]{1,0:T(8,128)(2,1)S(1)}, bf16[192,1024]{1,0:T(8,128)(2,1)}, u32[]{:S(2)}, u32[]{:S(2)}) collective-permute-start(bf16[192,1024]{1,0:T(8,128)(2,1)S(1)} %slice.12), channel_id=1, source_target_pairs={{0,1},{1,0},{2,3},{3,2},{4,5},{5,4},{6,7},{7,6},{8,9},{9,8},{10,11... | collective-permute-start | bytes 1179656 | tf_op jit(solution)/shard_map/ppermute | solution.py:326
  11.3 1.8 slice.13
  13.2 2.3 slice.14
  15.4 1.9 slice.15
  17.3 3.2 %collective-permute-done.refs_0_ = bf16[192,1024]{1,0:T(8,128)(2,1)} collective-permute-done((bf16[192,1024]{1,0:T(8,128)(2,1)S(1)}, bf16[192,1024]{1,0:T(8,128)(2,1)}, u32[]{:S(2)}, u32[]{:S(2)}) %collective-permute-start) | collective-permute-done | bytes 393248 | tf_op jit(solution)/shard_map/ppermute | solution.py:326
  20.6 1.7 collective-permute-start.4
  22.3 47.9 %collective-permute-done.4.refs_1_ = bf16[1088,1024]{1,0:T(8,128)(2,1)S(1)} collective-permute-done((bf16[1088,1024]{1,0:T(8,128)(2,1)S(1)}, bf16[1088,1024]{1,0:T(8,128)(2,1)S(1)}, u32[]{:S(2)}, u32[]{:S(2)}) %collective-permute-start.4) | collective-permute-done | bytes 2228256 | tf_op jit(solution)/shard_map/ppermute | solution.py:326
  70.2 0.0 collective-permute-start.7
  70.2 3.7 %collective-permute-start.1 = (bf16[512,1024]{1,0:T(8,128)(2,1)}, bf16[512,1024]{1,0:T(8,128)(2,1)S(1)}, u32[]{:S(2)}, u32[]{:S(2)}) collective-permute-start(bf16[512,1024]{1,0:T(8,128)(2,1)} %slice.14), channel_id=1, source_target_pairs={{0,1},{1,0},{2,3},{3,2},{4,5},{5,4},{6,7},{7,6},{8,9},{9,8},{10,11... | collective-permute-start | bytes 3145736 | tf_op jit(solution)/shard_map/ppermute | solution.py:326
  73.9 0.0 collective-permute-start.3
  73.9 0.0 collective-permute-start.6
  74.0 2.0 all-gather.3.cloned.1.call-done.w_ref.refs_2_
  76.0 18.3 %project_qkv.1 = (bf16[2048,1024]{1,0:T(8,128)(2,1)}, bf16[6144,1024]{1,0:T(8,128)(2,1)}, bf16[1024,6144]{1,0:T(8,128)(2,1)}) custom-call(bf16[2048,1024]{1,0:T(8,128)(2,1)} %x_ref.1, bf16[1024,3072]{1,0:T(8,128)(2,1)} %all-gather.3.cloned.1.call-done.w_ref.refs_2_), custom_call_target="tpu_custom_call" | custom-call | flops 12884901888 | bytes 16777216 | tf_op jit(solution)/shard_map/project_qkv/pallas_call | solution.py:47
  94.3 3.8 %collective-permute-done.1.refs_0_ = bf16[512,1024]{1,0:T(8,128)(2,1)S(1)} collective-permute-done((bf16[512,1024]{1,0:T(8,128)(2,1)}, bf16[512,1024]{1,0:T(8,128)(2,1)S(1)}, u32[]{:S(2)}, u32[]{:S(2)}) %collective-permute-start.1) | collective-permute-done | bytes 1048608 | tf_op jit(solution)/shard_map/ppermute | solution.py:326
  98.1 0.0 collective-permute-start.2
  98.1 8.6 %project_kv_halo.4 = (bf16[6144,1024]{1,0:T(8,128)(2,1)}, bf16[1024,6144]{1,0:T(8,128)(2,1)}) custom-call(bf16[192,1024]{1,0:T(8,128)(2,1)} %collective-permute-done.refs_0_, bf16[1088,1024]{1,0:T(8,128)(2,1)S(1)} %collective-permute-done.4.refs_1_, bf16[1024,3072]{1,0:T(8,128)(2,1)S(1)} %copy-done.1, ...), custom_call_target="tpu_custom_call", output_to_operand_aliasing={{0}: (3, {}), {1}: (4, {})} | custom-call | flops 5368709120 | bytes 7864320 | tf_op jit(solution)/shard_map/project_kv_halo/pallas_call | solution.py:102
  106.8 1.6 collective-permute-done.3.refs_1_
  108.4 0.0 collective-permute-start.5
  108.4 0.0 collective-permute-done.6.refs_0_
  108.4 9.3 %project_kv_halo.5 = (bf16[6144,1024]{1,0:T(8,128)(2,1)}, bf16[1024,6144]{1,0:T(8,128)(2,1)}) custom-call(bf16[192,1024]{1,0:T(8,128)(2,1)} %collective-permute-done.6.refs_0_, bf16[1088,1024]{1,0:T(8,128)(2,1)} %collective-permute-done.7.refs_1_, bf16[1024,3072]{1,0:T(8,128)(2,1)S(1)} %copy-done.1, ...), custom_call_target="tpu_custom_call", output_to_operand_aliasing={{0}: (3, {}), {1}: (4, {})} | custom-call | flops 5368709120 | bytes 7864320 | tf_op jit(solution)/shard_map/project_kv_halo/pallas_call | solution.py:102
  117.7 5.9 %project_kv_halo.6 = (bf16[6144,1024]{1,0:T(8,128)(2,1)}, bf16[1024,6144]{1,0:T(8,128)(2,1)}) custom-call(bf16[512,1024]{1,0:T(8,128)(2,1)S(1)} %collective-permute-done.1.refs_0_, bf16[256,1024]{1,0:T(8,128)(2,1)} %collective-permute-done.3.refs_1_, bf16[1024,3072]{1,0:T(8,128)(2,1)S(1)} %copy-done.1, ...), custom_call_target="tpu_custom_call", output_to_operand_aliasing={{0}: (3, {}), {1}: (4, {})} | custom-call | flops 3221225472 | bytes 4718592 | tf_op jit(solution)/shard_map/project_kv_halo/pallas_call | solution.py:102
  123.5 0.0 collective-permute-done.2.refs_0_
  123.6 4.8 %project_kv_halo.7 = (bf16[6144,1024]{1,0:T(8,128)(2,1)}, bf16[1024,6144]{1,0:T(8,128)(2,1)}) custom-call(bf16[512,1024]{1,0:T(8,128)(2,1)S(1)} %collective-permute-done.2.refs_0_, bf16[256,1024]{1,0:T(8,128)(2,1)S(1)} %collective-permute-done.5.refs_1_, bf16[1024,3072]{1,0:T(8,128)(2,1)S(1)} %copy-done.1, ...), custom_call_target="tpu_custom_call", output_to_operand_aliasing={{0}: (3, {}), {1}: (4, {})} | custom-call | flops 3221225472 | bytes 4718592 | tf_op jit(solution)/shard_map/project_kv_halo/pallas_call | solution.py:102
  128.4 0.0 all-gather.5.cloned.1.call-update
  128.4 0.1 constant_dynamic-slice_fusion
  128.5 0.1 copy.14
  128.6 0.6 fusion.4.lists_ref
  129.2 141.7 %attend.1.x_ref = bf16[2048,1024]{1,0:T(8,128)(2,1)} custom-call(s32[16,12]{1,0:T(8,128)} %fusion.4.lists_ref, bf16[2048,1024]{1,0:T(8,128)(2,1)} %get-tuple-element.30.q_ref, bf16[6144,1024]{1,0:T(8,128)(2,1)} %get-tuple-element.52.k_ref, bf16[1024,6144]{1,0:T(8,128)(2,1)} %get-tuple-element.53.vt_ref), custom_call_target="tpu_custom_call" | custom-call | flops 12884901888 | bytes 33554432 | tf_op jit(solution)/shard_map/attend/pallas_call | solution.py:254
  270.9 10.0 %project_update.1 = bf16[2048,1024]{1,0:T(8,128)(2,1)} custom-call(bf16[2048,1024]{1,0:T(8,128)(2,1)} %attend.1.x_ref, bf16[1024,1024]{1,0:T(8,128)(2,1)} %all-gather.5.cloned.1.call-done.w_ref), custom_call_target="tpu_custom_call" | custom-call | flops 4294967296 | bytes 8388608 | tf_op jit(solution)/shard_map/project_update/pallas_call | solution.py:130
  (8 shorter events, 0.0 us)
Async XLA Ops:
  6.5 121.9 %copy-start = (s32[32,12]{0,1:T(8,128)S(1)}, s32[32,12]{0,1:T(8,128)}, u32[]{:S(2)}) copy-start(s32[32,12]{0,1:T(8,128)} %param.7) | copy-start | bytes 4612
  6.5 69.4 %all-gather.3.cloned.1.call-start = ((), (), s32[]{:S(2)}) async-start(), calls=%async_computation | async-start | bytes 6684672 | tf_op jit(solution)/shard_map/all_gather | solution.py:309
  7.3 263.6 %all-gather.5.cloned.1.call-start = ((), (), s32[]{:S(2)}) async-start(), calls=%async_computation.1 | async-start | bytes 2228224 | tf_op jit(solution)/shard_map/all_gather | solution.py:345
  8.3 12.2 %collective-permute-start = (bf16[192,1024]{1,0:T(8,128)(2,1)S(1)}, bf16[192,1024]{1,0:T(8,128)(2,1)}, u32[]{:S(2)}, u32[]{:S(2)}) collective-permute-start(bf16[192,1024]{1,0:T(8,128)(2,1)S(1)} %slice.12), channel_id=1, source_target_pairs={{0,1},{1,0},{2,3},{3,2},{4,5},{5,4},{6,7},{7,6},{8,9},{9,8},{10,11... | collective-permute-start | bytes 1179656 | tf_op jit(solution)/shard_map/ppermute | solution.py:326
  20.6 49.6 %collective-permute-start.4 = (bf16[1088,1024]{1,0:T(8,128)(2,1)S(1)}, bf16[1088,1024]{1,0:T(8,128)(2,1)S(1)}, u32[]{:S(2)}, u32[]{:S(2)}) collective-permute-start(bf16[1088,1024]{1,0:T(8,128)(2,1)S(1)} %slice.13), channel_id=1, source_target_pairs={{0,1},{1,0},{2,3},{3,2},{4,5},{5,4},{6,7},{7,6},{8,9},{9,8},{10,11... | collective-permute-start | bytes 6684680 | tf_op jit(solution)/shard_map/ppermute | solution.py:326
  70.2 38.2 %collective-permute-start.7 = (bf16[1088,1024]{1,0:T(8,128)(2,1)S(1)}, bf16[1088,1024]{1,0:T(8,128)(2,1)}, u32[]{:S(2)}, u32[]{:S(2)}) collective-permute-start(bf16[1088,1024]{1,0:T(8,128)(2,1)S(1)} %collective-permute-done.4.refs_1_), channel_id=1, source_target_pairs={{0,2},{1,31},{2,4},{3,1},{4,6},{5,3},{6,8},{7,5},{8,10},{9,7},{10,... | collective-permute-start | bytes 6684680 | tf_op jit(solution)/shard_map/ppermute | solution.py:300
  70.2 28.0 %collective-permute-start.1 = (bf16[512,1024]{1,0:T(8,128)(2,1)}, bf16[512,1024]{1,0:T(8,128)(2,1)S(1)}, u32[]{:S(2)}, u32[]{:S(2)}) collective-permute-start(bf16[512,1024]{1,0:T(8,128)(2,1)} %slice.14), channel_id=1, source_target_pairs={{0,1},{1,0},{2,3},{3,2},{4,5},{5,4},{6,7},{7,6},{8,9},{9,8},{10,11... | collective-permute-start | bytes 3145736 | tf_op jit(solution)/shard_map/ppermute | solution.py:326
  73.9 34.4 %collective-permute-start.3 = (bf16[256,1024]{1,0:T(8,128)(2,1)}, bf16[256,1024]{1,0:T(8,128)(2,1)}, u32[]{:S(2)}, u32[]{:S(2)}) collective-permute-start(bf16[256,1024]{1,0:T(8,128)(2,1)} %slice.15), channel_id=1, source_target_pairs={{0,1},{1,0},{2,3},{3,2},{4,5},{5,4},{6,7},{7,6},{8,9},{9,8},{10,11... | collective-permute-start | bytes 1572872 | tf_op jit(solution)/shard_map/ppermute | solution.py:326
  73.9 34.4 %collective-permute-start.6 = (bf16[192,1024]{1,0:T(8,128)(2,1)}, bf16[192,1024]{1,0:T(8,128)(2,1)}, u32[]{:S(2)}, u32[]{:S(2)}) collective-permute-start(bf16[192,1024]{1,0:T(8,128)(2,1)} %collective-permute-done.refs_0_), channel_id=1, source_target_pairs={{0,2},{1,31},{2,4},{3,1},{4,6},{5,3},{6,8},{7,5},{8,10},{9,7},{10,... | collective-permute-start | bytes 1179656 | tf_op jit(solution)/shard_map/ppermute | solution.py:300
  76.0 22.2 %copy-start.1 = (bf16[1024,3072]{1,0:T(8,128)(2,1)S(1)}, bf16[1024,3072]{1,0:T(8,128)(2,1)}, u32[]{:S(2)}) copy-start(bf16[1024,3072]{1,0:T(8,128)(2,1)} %all-gather.3.cloned.1.call-done.w_ref.refs_2_) | copy-start | bytes 18874372
  98.1 25.4 %collective-permute-start.2 = (bf16[512,1024]{1,0:T(8,128)(2,1)S(1)}, bf16[512,1024]{1,0:T(8,128)(2,1)S(1)}, u32[]{:S(2)}, u32[]{:S(2)}) collective-permute-start(bf16[512,1024]{1,0:T(8,128)(2,1)S(1)} %collective-permute-done.1.refs_0_), channel_id=1, source_target_pairs={{0,2},{1,31},{2,4},{3,1},{4,6},{5,3},{6,8},{7,5},{8,10},{9,7},{10,... | collective-permute-start | bytes 3145736 | tf_op jit(solution)/shard_map/ppermute | solution.py:300
  108.4 15.2 %collective-permute-start.5 = (bf16[256,1024]{1,0:T(8,128)(2,1)}, bf16[256,1024]{1,0:T(8,128)(2,1)S(1)}, u32[]{:S(2)}, u32[]{:S(2)}) collective-permute-start(bf16[256,1024]{1,0:T(8,128)(2,1)} %collective-permute-done.3.refs_1_), channel_id=1, source_target_pairs={{0,2},{1,31},{2,4},{3,1},{4,6},{5,3},{6,8},{7,5},{8,10},{9,7},{10,... | collective-permute-start | bytes 1572872 | tf_op jit(solution)/shard_map/ppermute | solution.py:300
Sparse Core Ops, SparseCore 0:
  9.6 66.2 all-gather.2
  128.5 41.5 all-gather.4

commit v4 on v3

--- a/solution.py
+++ b/solution.py
@@ -16,24 +16,56 @@
 D = HEADS * HD
 PLANE = PB * BLK
 TILE = 512
-UPDATE_TILE = 256
-CUTS = (192, 1088, 512, 256)
+CUTS = (1280, 640, 128)
+STEP = 512
 LARGE = 2.0**100
 MIB = 1 << 20
 VMEM_LIMIT = 54 * MIB
 
 
-def project_own_kernel(x_ref, w_ref, q_ref, k_ref, vt_ref):
-    x = x_ref[...]
-
-    def part(start):
-        product = jnp.dot(x, w_ref[:, start : start + 512], preferred_element_type=jnp.float32)
-        return product.astype(jnp.bfloat16)
-
-    for col in range(0, D, 512):
-        q_ref[:, col : col + 512] = part(col)
-        k_ref[:, col : col + 512] = part(D + col)
-        vt_ref[col : col + 512, :] = part(2 * D + col).T
+def project_own_kernel(x_ref, other_ref, w_hbm, q_hbm, k_hbm, vt_hbm, *scratch):
+    w_ref, q_ref, k_ref, vt_ref, w_sem, q_sem, k_sem, vt_sem = scratch
+    loads = []
+    for i in range(3 * D // STEP):
+        columns = pl.ds(i * STEP, STEP)
+        loads.append(
+            pltpu.make_async_copy(w_hbm.at[:, columns], w_ref.at[:, columns], w_sem.at[i])
+        )
+        loads[-1].start()
+    pending = set(range(len(loads)))
+    own = x_ref.shape[0]
+    total = own + other_ref.shape[0]
+    copies = []
+
+    def send(source, target, sem):
+        copies.append(pltpu.make_async_copy(source, target, sem))
+        copies[-1].start()
+
+    for i, start in enumerate(range(0, total, TILE)):
+        stop = min(start + TILE, total)
+        rows = slice(start, stop)
+        x = x_ref[rows, :] if start < own else other_ref[start - own : stop - own, :]
+
+        def part(index, x=x):
+            if index in pending:
+                pending.remove(index)
+                loads[index].wait()
+            weights = w_ref[:, index * STEP : (index + 1) * STEP]
+            return jnp.dot(x, weights, preferred_element_type=jnp.float32).astype(jnp.bfloat16)
+
+        third = D // STEP
+        if start < own:
+            for j in range(third):
+                q_ref[rows, j * STEP : (j + 1) * STEP] = part(j)
+            send(q_ref.at[rows, :], q_hbm.at[rows, :], q_sem.at[i])
+        for j in range(third):
+            k_ref[rows, j * STEP : (j + 1) * STEP] = part(third + j)
+        send(k_ref.at[rows, :], k_hbm.at[rows, :], k_sem.at[i])
+        for j in range(third):
+            vt_ref[j * STEP : (j + 1) * STEP, rows] = part(2 * third + j).T
+        send(vt_ref.at[:, rows], vt_hbm.at[:, rows], vt_sem.at[i])
+    for copy in copies:
+        copy.wait()
 
 
 def project_cost(rows, columns):
@@ -42,22 +74,35 @@
     )
 
 
-def project_own(x, w):
-    row_spec = pl.BlockSpec((TILE, D), lambda i: (i, 0))
+def project_own(x, other, w):
+    own = x.shape[0]
+    total = own + other.shape[0]
+    tiles = -(-total // TILE)
+    vmem = pl.BlockSpec(memory_space=pltpu.VMEM)
+    hbm = pl.BlockSpec(memory_space=pltpu.HBM)
     return pl.pallas_call(
         project_own_kernel,
-        grid=(PLANE // TILE,),
-        in_specs=[row_spec, pl.BlockSpec(memory_space=pltpu.VMEM)],
-        out_specs=[row_spec, row_spec, pl.BlockSpec((D, TILE), lambda i: (0, i))],
+        in_specs=[vmem, vmem, hbm],
+        out_specs=[hbm, hbm, hbm],
         out_shape=[
-            jax.ShapeDtypeStruct((PLANE, D), jnp.bfloat16),
+            jax.ShapeDtypeStruct((own, D), jnp.bfloat16),
             jax.ShapeDtypeStruct((3 * PLANE, D), jnp.bfloat16),
             jax.ShapeDtypeStruct((D, 3 * PLANE), jnp.bfloat16),
         ],
-        compiler_params=pltpu.CompilerParams(vmem_limit_bytes=VMEM_LIMIT),
-        cost_estimate=project_cost(PLANE, 3 * D),
+        scratch_shapes=[
+            pltpu.VMEM((D, 3 * D), jnp.bfloat16),
+            pltpu.VMEM((own, D), jnp.bfloat16),
+            pltpu.VMEM((total, D), jnp.bfloat16),
+            pltpu.VMEM((D, total), jnp.bfloat16),
+            pltpu.SemaphoreType.DMA((3 * D // STEP,)),
+            pltpu.SemaphoreType.DMA((tiles,)),
+            pltpu.SemaphoreType.DMA((tiles,)),
+            pltpu.SemaphoreType.DMA((tiles,)),
+        ],
+        compiler_params=pltpu.CompilerParams(vmem_limit_bytes=48 * MIB),
+        cost_estimate=project_cost(total, 3 * D),
         name="project_qkv",
-    )(x, w)
+    )(x, other, w)
 
 
 def project_halo_kernel(counts, bases, *refs):
@@ -121,20 +166,20 @@
 
 
 def update_kernel(x_ref, w_ref, o_ref):
-    part = jnp.dot(x_ref[...], w_ref[...], preferred_element_type=jnp.float32)
-    o_ref[...] = part.astype(jnp.bfloat16)
+    x = x_ref[...]
+    for col in range(0, D, STEP):
+        part = jnp.dot(x, w_ref[:, col : col + STEP], preferred_element_type=jnp.float32)
+        o_ref[:, col : col + STEP] = part.astype(jnp.bfloat16)
 
 
 def project_update(x, w):
     rows = x.shape[0]
+    row_spec = pl.BlockSpec((TILE, D), lambda i: (i, 0))
     return pl.pallas_call(
         update_kernel,
-        grid=(rows // UPDATE_TILE,),
-        in_specs=[
-            pl.BlockSpec((UPDATE_TILE, D), lambda i: (i, 0)),
-            pl.BlockSpec((D, D), lambda i: (0, 0), pipeline_mode=pl.Buffered(1)),
-        ],
-        out_specs=pl.BlockSpec((UPDATE_TILE, D), lambda i: (i, 0)),
+        grid=(rows // TILE,),
+        in_specs=[row_spec, pl.BlockSpec(memory_space=pltpu.VMEM)],
+        out_specs=row_spec,
         out_shape=jax.ShapeDtypeStruct((rows, D), jnp.bfloat16),
         compiler_params=pltpu.CompilerParams(vmem_limit_bytes=VMEM_LIMIT),
         cost_estimate=project_cost(rows, D),
@@ -313,8 +358,8 @@
         own = lax.dynamic_slice_in_dim(slab, side * PLANE, PLANE, axis=0)
         other = lax.dynamic_slice_in_dim(slab, (1 - side) * PLANE, PLANE, axis=0)
         far = forward(other)
-        q, k, vt = project_own(own, w)
-        k, vt = project_halo([([other], PLANE)], w, k, vt)
+        q, k, vt = project_own(own, other, w)
+        k, w_last = tie((k, w_out))
         k, vt = project_halo([([far], 2 * PLANE)], w, k, vt)
         q = lax.dynamic_slice_in_dim(q, head % per_plane * rows, rows, axis=0)
     else:
@@ -330,18 +375,13 @@
         x_0 = swap(first)
         later = [rest[start:stop] for start, stop in zip(cuts[1:], cuts[2:])]
         x_0, *later = tie((x_0, *later))
-        x_1, x_2, x_3 = [swap(part) for part in later]
-        far_0, far_1 = forward(x_0), forward(x_1)
-        q, k, vt = project_own(tokens, w)
-        x_2, k, vt = tie((x_2, k, vt))
-        far_2 = forward(x_2)
-        k, vt = project_halo([([x_0, x_1], PLANE)], w, k, vt)
-        x_3, k, vt = tie((x_3, k, vt))
-        far_3 = forward(x_3)
-        k, vt = project_halo([([far_0, far_1], 2 * PLANE)], w, k, vt)
-        k, vt = project_halo([([x_2, x_3], PLANE + cuts[2])], w, k, vt)
-        k, vt = project_halo([([far_2, far_3], 2 * PLANE + cuts[2])], w, k, vt)
-    k, w_last = tie((k, w_out))
+        x_1, x_2 = [swap(part) for part in later]
+        far_0 = forward(x_0)
+        q, k, vt = project_own(tokens, x_0, w)
+        x_1, x_2, k, vt, w_last = tie((x_1, x_2, k, vt, w_out))
+        far_1, far_2 = forward(x_1), forward(x_2)
+        k, vt = project_halo([([far_0], 2 * PLANE), ([x_1, x_2], PLANE + cuts[1])], w, k, vt)
+        k, vt = project_halo([([far_1, far_2], 2 * PLANE + cuts[1])], w, k, vt)
     w_last = lax.all_gather(w_last, "seq", axis=0, tiled=True)
     attended = attend(lists, q, k, vt, 0, blocks)
     return project_update(attended, w_last)

time: 290 us -> 296 us (1.021)
  waiting for transfers between devices: 59.3 us -> 72.5 us
  Pallas kernels: 199 us -> 193 us
    pallas_call x4 -> x2, Pallas kernels: 28.5 us -> 17.7 us  [project_halo(): pl.pallas_call(functools.partial(project_halo_kernel, counts, bases), in_...]
    ppermute x4 -> x3, waiting for transfers between devices: 0.01 us -> 10.1 us  [forward(): return lax.ppermute(x, ('seq', 'head'), hops)]
    pallas_call x2, Pallas kernels: 28.3 us -> 34 us  [the longest x1 25.6 us: project_own(): pl.pallas_call(project_own_kernel, in_specs=[vmem, vmem, hbm], out_specs=...]
    all_gather x1, waiting for transfers between devices: 2.03 us -> 5.59 us  [local(): w = lax.all_gather(w_qkv, 'seq', axis=0, tiled=True)]
    ppermute x4 -> x3, starting transfers between devices: 8.5 us -> 5.03 us  [swap(): return lax.ppermute(x, 'head', [(0, 1), (1, 0)])]
    slice x3 -> x2, local copies, waits for them, and re-layouts: 5.98 us -> 3.46 us  [local(): later = [rest[start:stop] for start, stop in zip(cuts[1:], cuts[2:])]]
    ppermute x4 -> x3, waiting for transfers between devices: 56.5 us -> 56 us  [swap(): return lax.ppermute(x, 'head', [(0, 1), (1, 0)])]
  transfers between devices with their start and end apart: 10 -> 8, of which waited for: 5 -> 4; matrix products, arithmetic and copies ran while one was open for 3% -> 2% of each run, Pallas kernels for 64% -> 63%
where the time goes in v4:
time: 296 us; the launch traced here: 295 us
  Pallas kernels  193 us (65%)
  waiting for transfers between devices  72.5 us (24%)
  between operations  13.5 us (5%)
  local copies, waits for them, and re-layouts  8.39 us (3%)
  starting transfers between devices  6.66 us (2%)
    pallas_call x1, Pallas kernels, attend(): pl.pallas_call(functools.partial(attend_kernel, first, blocks), grid_spec...  142 us
    ppermute x3, waiting for transfers between devices, swap(): return lax.ppermute(x, 'head', [(0, 1), (1, 0)])  56 us
    pallas_call x1, Pallas kernels, project_own(): pl.pallas_call(project_own_kernel, in_specs=[vmem, vmem, hbm], out_specs=...  25.6 us
    pallas_call x2, Pallas kernels, project_halo(): pl.pallas_call(functools.partial(project_halo_kernel, counts, bases), in_...  17.7 us
    ppermute x3, waiting for transfers between devices, forward(): return lax.ppermute(x, ('seq', 'head'), hops)  10.1 us
    pallas_call x1, Pallas kernels, project_update(): pl.pallas_call(update_kernel, grid=(rows // TILE,), in_specs=[row_spec, p...  8.36 us
  transfers between devices with their start and end apart: 8, of which 4 were waited for; matrix products, arithmetic and copies ran while one was open for 2% of the time, Pallas kernels for 63%

profile of v4, /device:TPU:0, one launch (start us, length us, event | category | flops | bytes accessed | tf_op | source)
XLA Modules:
  0.0 295.0 jit_solution(18375346603905509148)
XLA Ops:
  6.5 0.0 copy-start
  6.5 0.0 all-gather.3.cloned.1.call-start
  6.5 0.7 all-gather.3.cloned.1.call-update
  7.3 0.0 all-gather.5.cloned.1.call-start
  7.3 2.0 slice.9
  9.3 3.0 %collective-permute-start = (bf16[1280,1024]{1,0:T(8,128)(2,1)S(1)}, bf16[1280,1024]{1,0:T(8,128)(2,1)}, u32[]{:S(2)}, u32[]{:S(2)}) collective-permute-start(bf16[1280,1024]{1,0:T(8,128)(2,1)S(1)} %slice.9), channel_id=1, source_target_pairs={{0,1},{1,0},{2,3},{3,2},{4,5},{5,4},{6,7},{7,6},{8,9},{9,8},{10,11... | collective-permute-start | bytes 7864328 | tf_op jit(solution)/shard_map/ppermute | solution.py:371
  12.3 2.5 slice.10
  14.8 1.0 slice.11
  15.8 53.5 %collective-permute-done.other_ref = bf16[1280,1024]{1,0:T(8,128)(2,1)} collective-permute-done((bf16[1280,1024]{1,0:T(8,128)(2,1)S(1)}, bf16[1280,1024]{1,0:T(8,128)(2,1)}, u32[]{:S(2)}, u32[]{:S(2)}) %collective-permute-start) | collective-permute-done | bytes 2621472 | tf_op jit(solution)/shard_map/ppermute | solution.py:371
  69.3 1.7 collective-permute-start.1
  71.0 0.3 collective-permute-start.2
  71.3 0.0 collective-permute-start.5
  71.3 5.6 %all-gather.3.cloned.1.call-done.w_hbm.refs_3_.refs_2_ = bf16[1024,3072]{1,0:T(8,128)(2,1)} async-done(((bf16[64,3072]{1,0:T(8,128)(2,1)}), bf16[1024,3072]{1,0:T(8,128)(2,1)}) %all-gather.3.cloned.1.call-update) | async-done | bytes 6291472 | tf_op jit(solution)/shard_map/all_gather | solution.py:354
  76.9 25.6 %project_qkv.1 = (bf16[2048,1024]{1,0:T(8,128)(2,1)}, bf16[6144,1024]{1,0:T(8,128)(2,1)}, bf16[1024,6144]{1,0:T(8,128)(2,1)}) custom-call(bf16[2048,1024]{1,0:T(8,128)(2,1)} %x_ref.1, bf16[1280,1024]{1,0:T(8,128)(2,1)} %collective-permute-done.other_ref, bf16[1024,3072]{1,0:T(8,128)(2,1)} %all-gather.3.cloned.1.call-done.w_hbm.refs_3_.refs_2_), custom_call_target="tpu_custom_call" | custom-call | flops 20937965568 | bytes 27262976 | tf_op jit(solution)/shard_map/project_qkv/pallas_call | solution.py:83
  102.5 2.5 collective-permute-done.2.refs_2_
  105.1 0.0 collective-permute-done.1.refs_1_
  105.1 0.0 all-gather.5.cloned.1.call-update
  105.1 0.1 collective-permute-start.3
  105.2 0.0 copy-done
  105.2 0.1 constant_dynamic-slice_fusion
  105.2 0.1 copy.10
  105.3 0.6 fusion.4.lists_ref
  106.0 1.5 collective-permute-start.4
  107.5 0.0 collective-permute-done.5.refs_0_
  107.5 0.0 copy-start.1
  107.5 2.8 copy-done.1
  110.3 11.7 %project_kv_halo.2 = (bf16[6144,1024]{1,0:T(8,128)(2,1)}, bf16[1024,6144]{1,0:T(8,128)(2,1)}) custom-call(bf16[1280,1024]{1,0:T(8,128)(2,1)S(1)} %collective-permute-done.5.refs_0_, bf16[640,1024]{1,0:T(8,128)(2,1)} %collective-permute-done.1.refs_1_, ...), custom_call_target="tpu_custom_call", output_to_operand_aliasing={{0}: (4, {}), {1}: (5, {})} | custom-call | flops 8589934592 | bytes 12582912 | tf_op jit(solution)/shard_map/project_kv_halo/pallas_call | solution.py:147
  122.0 10.1 %collective-permute-done.4.refs_1_ = bf16[128,1024]{1,0:T(8,128)(2,1)S(1)} collective-permute-done((bf16[128,1024]{1,0:T(8,128)(2,1)S(1)}, bf16[128,1024]{1,0:T(8,128)(2,1)S(1)}, u32[]{:S(2)}, u32[]{:S(2)}) %collective-permute-start.4) | collective-permute-done | bytes 262176 | tf_op jit(solution)/shard_map/ppermute | solution.py:345
  132.1 0.0 collective-permute-done.3.refs_0_
  132.1 6.0 %project_kv_halo.3 = (bf16[6144,1024]{1,0:T(8,128)(2,1)}, bf16[1024,6144]{1,0:T(8,128)(2,1)}) custom-call(bf16[640,1024]{1,0:T(8,128)(2,1)} %collective-permute-done.3.refs_0_, bf16[128,1024]{1,0:T(8,128)(2,1)S(1)} %collective-permute-done.4.refs_1_, bf16[1024,3072]{1,0:T(8,128)(2,1)S(1)} %copy-done.1, ...), custom_call_target="tpu_custom_call", output_to_operand_aliasing={{0}: (3, {}), {1}: (4, {})} | custom-call | flops 3221225472 | bytes 4718592 | tf_op jit(solution)/shard_map/project_kv_halo/pallas_call | solution.py:147
  138.2 141.7 %attend.1.x_ref = bf16[2048,1024]{1,0:T(8,128)(2,1)} custom-call(s32[16,12]{1,0:T(8,128)} %fusion.4.lists_ref, bf16[2048,1024]{1,0:T(8,128)(2,1)} %get-tuple-element.25.q_ref, bf16[6144,1024]{1,0:T(8,128)(2,1)} %get-tuple-element.36.k_ref, bf16[1024,6144]{1,0:T(8,128)(2,1)} %get-tuple-element.37.vt_ref), custom_call_target="tpu_custom_call" | custom-call | flops 12884901888 | bytes 33554432 | tf_op jit(solution)/shard_map/attend/pallas_call | solution.py:299
  279.8 8.4 %project_update.1 = bf16[2048,1024]{1,0:T(8,128)(2,1)} custom-call(bf16[2048,1024]{1,0:T(8,128)(2,1)} %attend.1.x_ref, bf16[1024,1024]{1,0:T(8,128)(2,1)} %all-gather.5.cloned.1.call-done.w_ref), custom_call_target="tpu_custom_call" | custom-call | flops 4294967296 | bytes 8388608 | tf_op jit(solution)/shard_map/project_update/pallas_call | solution.py:178
  (1 shorter events, 0.0 us)
Async XLA Ops:
  6.5 98.6 %copy-start = (s32[32,12]{0,1:T(8,128)S(1)}, s32[32,12]{0,1:T(8,128)}, u32[]{:S(2)}) copy-start(s32[32,12]{0,1:T(8,128)} %param.7) | copy-start | bytes 4612
  6.5 70.3 %all-gather.3.cloned.1.call-start = ((), (), s32[]{:S(2)}) async-start(), calls=%async_computation | async-start | bytes 6684672 | tf_op jit(solution)/shard_map/all_gather | solution.py:354
  7.3 272.6 %all-gather.5.cloned.1.call-start = ((), (), s32[]{:S(2)}) async-start(), calls=%async_computation.1 | async-start | bytes 2228224 | tf_op jit(solution)/shard_map/all_gather | solution.py:385
  9.3 60.0 %collective-permute-start = (bf16[1280,1024]{1,0:T(8,128)(2,1)S(1)}, bf16[1280,1024]{1,0:T(8,128)(2,1)}, u32[]{:S(2)}, u32[]{:S(2)}) collective-permute-start(bf16[1280,1024]{1,0:T(8,128)(2,1)S(1)} %slice.9), channel_id=1, source_target_pairs={{0,1},{1,0},{2,3},{3,2},{4,5},{5,4},{6,7},{7,6},{8,9},{9,8},{10,11... | collective-permute-start | bytes 7864328 | tf_op jit(solution)/shard_map/ppermute | solution.py:371
  69.3 35.8 %collective-permute-start.1 = (bf16[640,1024]{1,0:T(8,128)(2,1)}, bf16[640,1024]{1,0:T(8,128)(2,1)}, u32[]{:S(2)}, u32[]{:S(2)}) collective-permute-start(bf16[640,1024]{1,0:T(8,128)(2,1)} %slice.10), channel_id=1, source_target_pairs={{0,1},{1,0},{2,3},{3,2},{4,5},{5,4},{6,7},{7,6},{8,9},{9,8},{10,11... | collective-permute-start | bytes 3932168 | tf_op jit(solution)/shard_map/ppermute | solution.py:371
  71.0 34.1 %collective-permute-start.2 = (bf16[128,1024]{1,0:T(8,128)(2,1)S(1)}, bf16[128,1024]{1,0:T(8,128)(2,1)S(1)}, u32[]{:S(2)}, u32[]{:S(2)}) collective-permute-start(bf16[128,1024]{1,0:T(8,128)(2,1)S(1)} %slice.11), channel_id=1, source_target_pairs={{0,1},{1,0},{2,3},{3,2},{4,5},{5,4},{6,7},{7,6},{8,9},{9,8},{10,11... | collective-permute-start | bytes 786440 | tf_op jit(solution)/shard_map/ppermute | solution.py:371
  71.3 36.2 %collective-permute-start.5 = (bf16[1280,1024]{1,0:T(8,128)(2,1)}, bf16[1280,1024]{1,0:T(8,128)(2,1)S(1)}, u32[]{:S(2)}, u32[]{:S(2)}) collective-permute-start(bf16[1280,1024]{1,0:T(8,128)(2,1)} %collective-permute-done.other_ref), channel_id=1, source_target_pairs={{0,2},{1,31},{2,4},{3,1},{4,6},{5,3},{6,8},{7,5},{8,10},{9,7},{10,... | collective-permute-start | bytes 7864328 | tf_op jit(solution)/shard_map/ppermute | solution.py:345
  105.1 27.0 %collective-permute-start.3 = (bf16[640,1024]{1,0:T(8,128)(2,1)}, bf16[640,1024]{1,0:T(8,128)(2,1)}, u32[]{:S(2)}, u32[]{:S(2)}) collective-permute-start(bf16[640,1024]{1,0:T(8,128)(2,1)} %collective-permute-done.1.refs_1_), channel_id=1, source_target_pairs={{0,2},{1,31},{2,4},{3,1},{4,6},{5,3},{6,8},{7,5},{8,10},{9,7},{10,... | collective-permute-start | bytes 3932168 | tf_op jit(solution)/shard_map/ppermute | solution.py:345
  106.0 26.1 %collective-permute-start.4 = (bf16[128,1024]{1,0:T(8,128)(2,1)S(1)}, bf16[128,1024]{1,0:T(8,128)(2,1)S(1)}, u32[]{:S(2)}, u32[]{:S(2)}) collective-permute-start(bf16[128,1024]{1,0:T(8,128)(2,1)S(1)} %collective-permute-done.2.refs_2_), channel_id=1, source_target_pairs={{0,2},{1,31},{2,4},{3,1},{4,6},{5,3},{6,8},{7,5},{8,10},{9,7},{10,... | collective-permute-start | bytes 786440 | tf_op jit(solution)/shard_map/ppermute | solution.py:345
  107.5 2.8 copy-start.1
Sparse Core Ops, SparseCore 0:
  9.6 67.1 all-gather.2
  105.2 47.7 all-gather.4

commit v5 on v3

--- a/solution.py
+++ b/solution.py
@@ -16,8 +16,8 @@
 D = HEADS * HD
 PLANE = PB * BLK
 TILE = 512
-UPDATE_TILE = 256
-CUTS = (192, 1088, 512, 256)
+CUTS = (1280, 512, 256)
+STEP = 512
 LARGE = 2.0**100
 MIB = 1 << 20
 VMEM_LIMIT = 54 * MIB
@@ -121,20 +121,20 @@
 
 
 def update_kernel(x_ref, w_ref, o_ref):
-    part = jnp.dot(x_ref[...], w_ref[...], preferred_element_type=jnp.float32)
-    o_ref[...] = part.astype(jnp.bfloat16)
+    x = x_ref[...]
+    for col in range(0, D, STEP):
+        part = jnp.dot(x, w_ref[:, col : col + STEP], preferred_element_type=jnp.float32)
+        o_ref[:, col : col + STEP] = part.astype(jnp.bfloat16)
 
 
 def project_update(x, w):
     rows = x.shape[0]
+    row_spec = pl.BlockSpec((TILE, D), lambda i: (i, 0))
     return pl.pallas_call(
         update_kernel,
-        grid=(rows // UPDATE_TILE,),
-        in_specs=[
-            pl.BlockSpec((UPDATE_TILE, D), lambda i: (i, 0)),
-            pl.BlockSpec((D, D), lambda i: (0, 0), pipeline_mode=pl.Buffered(1)),
-        ],
-        out_specs=pl.BlockSpec((UPDATE_TILE, D), lambda i: (i, 0)),
+        grid=(rows // TILE,),
+        in_specs=[row_spec, pl.BlockSpec(memory_space=pltpu.VMEM)],
+        out_specs=row_spec,
         out_shape=jax.ShapeDtypeStruct((rows, D), jnp.bfloat16),
         compiler_params=pltpu.CompilerParams(vmem_limit_bytes=VMEM_LIMIT),
         cost_estimate=project_cost(rows, D),
@@ -146,7 +146,7 @@
     s_ref, p_ref, m_ref, l_ref = scratch
     factor = math.log2(math.e) / math.sqrt(HD)
     unroll = 4
-    edges = (0, 2, 7, 12)
+    edges = (0, 2, 12)
     parts = len(edges) - 1
 
     def listed(position):
@@ -263,7 +263,7 @@
             ],
             out_specs=pl.BlockSpec((rows, pair), lambda i, lists: (0, i)),
             scratch_shapes=[
-                pltpu.VMEM((3, 5 * BLK, pair), jnp.float32),
+                pltpu.VMEM((2, 10 * BLK, pair), jnp.float32),
                 pltpu.VMEM((2, keys, pair), jnp.bfloat16),
                 pltpu.VMEM((2, 8, pair), jnp.float32),
                 pltpu.VMEM((1, pair), jnp.float32),
@@ -330,17 +330,16 @@
         x_0 = swap(first)
         later = [rest[start:stop] for start, stop in zip(cuts[1:], cuts[2:])]
         x_0, *later = tie((x_0, *later))
-        x_1, x_2, x_3 = [swap(part) for part in later]
-        far_0, far_1 = forward(x_0), forward(x_1)
+        x_1, x_2 = [swap(part) for part in later]
+        far_0 = forward(x_0)
         q, k, vt = project_own(tokens, w)
+        x_1, k, vt = tie((x_1, k, vt))
+        far_1 = forward(x_1)
+        k, vt = project_halo([([x_0], PLANE)], w, k, vt)
         x_2, k, vt = tie((x_2, k, vt))
         far_2 = forward(x_2)
-        k, vt = project_halo([([x_0, x_1], PLANE)], w, k, vt)
-        x_3, k, vt = tie((x_3, k, vt))
-        far_3 = forward(x_3)
-        k, vt = project_halo([([far_0, far_1], 2 * PLANE)], w, k, vt)
-        k, vt = project_halo([([x_2, x_3], PLANE + cuts[2])], w, k, vt)
-        k, vt = project_halo([([far_2, far_3], 2 * PLANE + cuts[2])], w, k, vt)
+        k, vt = project_halo([([far_0], 2 * PLANE), ([x_1, x_2], PLANE + cuts[1])], w, k, vt)
+        k, vt = project_halo([([far_1, far_2], 2 * PLANE + cuts[1])], w, k, vt)
     k, w_last = tie((k, w_out))
     w_last = lax.all_gather(w_last, "seq", axis=0, tiled=True)
     attended = attend(lists, q, k, vt, 0, blocks)

time: 290 us -> 285 us (0.983)
  Pallas kernels: 199 us -> 194 us
  waiting for transfers between devices: 59.3 us -> 62.4 us
    pallas_call x4 -> x3, Pallas kernels: 28.5 us -> 24.6 us  [project_halo(): pl.pallas_call(functools.partial(project_halo_kernel, counts, bases), in_...]
    ppermute x4 -> x3, waiting for transfers between devices: 56.5 us -> 59.3 us  [swap(): return lax.ppermute(x, 'head', [(0, 1), (1, 0)])]
    slice x3 -> x2, local copies, waits for them, and re-layouts: 5.98 us -> 4.13 us  [local(): later = [rest[start:stop] for start, stop in zip(cuts[1:], cuts[2:])]]
    ppermute x4 -> x3, starting transfers between devices: 8.5 us -> 8 us  [swap(): return lax.ppermute(x, 'head', [(0, 1), (1, 0)])]
  transfers between devices with their start and end apart: 10 -> 8, of which waited for: 5 -> 5; matrix products, arithmetic and copies ran while one was open for 3% -> 2% of each run, Pallas kernels for 64% -> 64%
where the time goes in v5:
time: 285 us
  Pallas kernels  194 us (68%)
  waiting for transfers between devices  62.4 us (22%)
  between operations  13.5 us (5%)
  starting transfers between devices  8.05 us (3%)
  local copies, waits for them, and re-layouts  6.28 us (2%)
    pallas_call x1, Pallas kernels, attend(): pl.pallas_call(functools.partial(attend_kernel, first, blocks), grid_spec...  143 us
    ppermute x3, waiting for transfers between devices, swap(): return lax.ppermute(x, 'head', [(0, 1), (1, 0)])  59.3 us
    pallas_call x3, Pallas kernels, project_halo(): pl.pallas_call(functools.partial(project_halo_kernel, counts, bases), in_...  24.6 us
    pallas_call x1, Pallas kernels, project_own(): pl.pallas_call(project_own_kernel, grid=(PLANE // TILE,), in_specs=[row_s...  18.4 us
    pallas_call x1, Pallas kernels, project_update(): pl.pallas_call(update_kernel, grid=(rows // TILE,), in_specs=[row_spec, p...  8.36 us
    ppermute x3, starting transfers between devices, swap(): return lax.ppermute(x, 'head', [(0, 1), (1, 0)])  8 us
  transfers between devices with their start and end apart: 8, of which 5 were waited for; matrix products, arithmetic and copies ran while one was open for 2% of the time, Pallas kernels for 64%

profile of v5, /device:TPU:0, one launch (start us, length us, event | category | flops | bytes accessed | tf_op | source)
XLA Modules:
  0.0 285.2 jit_solution(15493322091533146677)
XLA Ops:
  6.5 0.0 copy-start
  6.5 0.0 all-gather.3.cloned.1.call-start
  6.5 0.7 all-gather.3.cloned.1.call-update
  7.3 0.0 all-gather.5.cloned.1.call-start
  7.3 2.0 slice.9
  9.3 3.0 %collective-permute-start = (bf16[1280,1024]{1,0:T(8,128)(2,1)S(1)}, bf16[1280,1024]{1,0:T(8,128)(2,1)S(1)}, u32[]{:S(2)}, u32[]{:S(2)}) collective-permute-start(bf16[1280,1024]{1,0:T(8,128)(2,1)S(1)} %slice.9), channel_id=1, source_target_pairs={{0,1},{1,0},{2,3},{3,2},{4,5},{5,4},{6,7},{7,6},{8,9},{9,8},{10,11... | collective-permute-start | bytes 7864328 | tf_op jit(solution)/shard_map/ppermute | solution.py:326
  12.3 2.3 slice.10
  14.5 1.9 slice.11
  16.4 52.7 %collective-permute-done.refs_0_ = bf16[1280,1024]{1,0:T(8,128)(2,1)S(1)} collective-permute-done((bf16[1280,1024]{1,0:T(8,128)(2,1)S(1)}, bf16[1280,1024]{1,0:T(8,128)(2,1)S(1)}, u32[]{:S(2)}, u32[]{:S(2)}) %collective-permute-start) | collective-permute-done | bytes 2621472 | tf_op jit(solution)/shard_map/ppermute | solution.py:326
  69.2 0.0 collective-permute-start.5
  69.2 5.0 %collective-permute-start.1 = (bf16[512,1024]{1,0:T(8,128)(2,1)}, bf16[512,1024]{1,0:T(8,128)(2,1)}, u32[]{:S(2)}, u32[]{:S(2)}) collective-permute-start(bf16[512,1024]{1,0:T(8,128)(2,1)} %slice.10), channel_id=1, source_target_pairs={{0,1},{1,0},{2,3},{3,2},{4,5},{5,4},{6,7},{7,6},{8,9},{9,8},{10,11... | collective-permute-start | bytes 3145736 | tf_op jit(solution)/shard_map/ppermute | solution.py:326
  74.1 0.0 collective-permute-start.3
  74.2 1.0 all-gather.3.cloned.1.call-done.w_ref.refs_1_.refs_3_.refs_2_
  75.2 18.4 %project_qkv.1 = (bf16[2048,1024]{1,0:T(8,128)(2,1)}, bf16[6144,1024]{1,0:T(8,128)(2,1)}, bf16[1024,6144]{1,0:T(8,128)(2,1)}) custom-call(bf16[2048,1024]{1,0:T(8,128)(2,1)} %x_ref.1, bf16[1024,3072]{1,0:T(8,128)(2,1)} %all-gather.3.cloned.1.call-done.w_ref.refs_1_.refs_3_.refs_2_), custom_call_target="tpu_custom_call" | custom-call | flops 12884901888 | bytes 16777216 | tf_op jit(solution)/shard_map/project_qkv/pallas_call | solution.py:47
  93.5 5.0 %collective-permute-done.1.refs_1_ = bf16[512,1024]{1,0:T(8,128)(2,1)} collective-permute-done((bf16[512,1024]{1,0:T(8,128)(2,1)}, bf16[512,1024]{1,0:T(8,128)(2,1)}, u32[]{:S(2)}, u32[]{:S(2)}) %collective-permute-start.1) | collective-permute-done | bytes 1048608 | tf_op jit(solution)/shard_map/ppermute | solution.py:326
  98.5 0.0 collective-permute-start.2
  98.5 0.0 copy-done.1
  98.5 7.5 %project_kv_halo.3 = (bf16[6144,1024]{1,0:T(8,128)(2,1)}, bf16[1024,6144]{1,0:T(8,128)(2,1)}) custom-call(bf16[1280,1024]{1,0:T(8,128)(2,1)S(1)} %collective-permute-done.refs_0_, bf16[1024,3072]{1,0:T(8,128)(2,1)S(1)} %copy-done.1, bf16[6144,1024]{1,0:T(8,128)(2,1)} %get-tuple-element.36.refs_2_, ...), custom_call_target="tpu_custom_call", output_to_operand_aliasing={{0}: (2, {}), {1}: (3, {})} | custom-call | flops 5368709120 | bytes 7864320 | tf_op jit(solution)/shard_map/project_kv_halo/pallas_call | solution.py:102
  106.0 1.6 collective-permute-done.3.refs_2_
  107.6 0.0 collective-permute-start.4
  107.6 0.0 collective-permute-done.5.refs_0_
  107.6 12.4 %project_kv_halo.4 = (bf16[6144,1024]{1,0:T(8,128)(2,1)}, bf16[1024,6144]{1,0:T(8,128)(2,1)}) custom-call(bf16[1280,1024]{1,0:T(8,128)(2,1)} %collective-permute-done.5.refs_0_, bf16[512,1024]{1,0:T(8,128)(2,1)} %collective-permute-done.1.refs_1_, ...), custom_call_target="tpu_custom_call", output_to_operand_aliasing={{0}: (4, {}), {1}: (5, {})} | custom-call | flops 8589934592 | bytes 12582912 | tf_op jit(solution)/shard_map/project_kv_halo/pallas_call | solution.py:102
  119.9 1.3 collective-permute-done.4.refs_1_
  121.3 0.0 collective-permute-done.2.refs_0_
  121.3 4.8 %project_kv_halo.5 = (bf16[6144,1024]{1,0:T(8,128)(2,1)}, bf16[1024,6144]{1,0:T(8,128)(2,1)}) custom-call(bf16[512,1024]{1,0:T(8,128)(2,1)S(1)} %collective-permute-done.2.refs_0_, bf16[256,1024]{1,0:T(8,128)(2,1)S(1)} %collective-permute-done.4.refs_1_, bf16[1024,3072]{1,0:T(8,128)(2,1)S(1)} %copy-done.1, ...), custom_call_target="tpu_custom_call", output_to_operand_aliasing={{0}: (3, {}), {1}: (4, {})} | custom-call | flops 3221225472 | bytes 4718592 | tf_op jit(solution)/shard_map/project_kv_halo/pallas_call | solution.py:102
  126.1 0.0 all-gather.5.cloned.1.call-update
  126.1 0.0 copy-done
  126.1 0.1 constant_dynamic-slice_fusion
  126.2 0.1 copy.12
  126.3 0.6 fusion.4.lists_ref
  126.9 143.1 %attend.1.x_ref = bf16[2048,1024]{1,0:T(8,128)(2,1)} custom-call(s32[16,12]{1,0:T(8,128)} %fusion.4.lists_ref, bf16[2048,1024]{1,0:T(8,128)(2,1)} %get-tuple-element.27.q_ref, bf16[6144,1024]{1,0:T(8,128)(2,1)} %get-tuple-element.46.k_ref, bf16[1024,6144]{1,0:T(8,128)(2,1)} %get-tuple-element.47.vt_ref), custom_call_target="tpu_custom_call" | custom-call | flops 12884901888 | bytes 33554432 | tf_op jit(solution)/shard_map/attend/pallas_call | solution.py:254
  270.0 8.4 %project_update.1 = bf16[2048,1024]{1,0:T(8,128)(2,1)} custom-call(bf16[2048,1024]{1,0:T(8,128)(2,1)} %attend.1.x_ref, bf16[1024,1024]{1,0:T(8,128)(2,1)} %all-gather.5.cloned.1.call-done.w_ref), custom_call_target="tpu_custom_call" | custom-call | flops 4294967296 | bytes 8388608 | tf_op jit(solution)/shard_map/project_update/pallas_call | solution.py:133
  (2 shorter events, 0.0 us)
Async XLA Ops:
  6.5 119.6 %copy-start = (s32[32,12]{0,1:T(8,128)S(1)}, s32[32,12]{0,1:T(8,128)}, u32[]{:S(2)}) copy-start(s32[32,12]{0,1:T(8,128)} %param.7) | copy-start | bytes 4612
  6.5 68.6 %all-gather.3.cloned.1.call-start = ((), (), s32[]{:S(2)}) async-start(), calls=%async_computation | async-start | bytes 6684672 | tf_op jit(solution)/shard_map/all_gather | solution.py:309
  7.3 262.7 %all-gather.5.cloned.1.call-start = ((), (), s32[]{:S(2)}) async-start(), calls=%async_computation.1 | async-start | bytes 2228224 | tf_op jit(solution)/shard_map/all_gather | solution.py:344
  9.3 59.9 %collective-permute-start = (bf16[1280,1024]{1,0:T(8,128)(2,1)S(1)}, bf16[1280,1024]{1,0:T(8,128)(2,1)S(1)}, u32[]{:S(2)}, u32[]{:S(2)}) collective-permute-start(bf16[1280,1024]{1,0:T(8,128)(2,1)S(1)} %slice.9), channel_id=1, source_target_pairs={{0,1},{1,0},{2,3},{3,2},{4,5},{5,4},{6,7},{7,6},{8,9},{9,8},{10,11... | collective-permute-start | bytes 7864328 | tf_op jit(solution)/shard_map/ppermute | solution.py:326
  69.2 38.4 %collective-permute-start.5 = (bf16[1280,1024]{1,0:T(8,128)(2,1)S(1)}, bf16[1280,1024]{1,0:T(8,128)(2,1)}, u32[]{:S(2)}, u32[]{:S(2)}) collective-permute-start(bf16[1280,1024]{1,0:T(8,128)(2,1)S(1)} %collective-permute-done.refs_0_), channel_id=1, source_target_pairs={{0,2},{1,31},{2,4},{3,1},{4,6},{5,3},{6,8},{7,5},{8,10},{9,7},{10,... | collective-permute-start | bytes 7864328 | tf_op jit(solution)/shard_map/ppermute | solution.py:300
  69.2 29.4 %collective-permute-start.1 = (bf16[512,1024]{1,0:T(8,128)(2,1)}, bf16[512,1024]{1,0:T(8,128)(2,1)}, u32[]{:S(2)}, u32[]{:S(2)}) collective-permute-start(bf16[512,1024]{1,0:T(8,128)(2,1)} %slice.10), channel_id=1, source_target_pairs={{0,1},{1,0},{2,3},{3,2},{4,5},{5,4},{6,7},{7,6},{8,9},{9,8},{10,11... | collective-permute-start | bytes 3145736 | tf_op jit(solution)/shard_map/ppermute | solution.py:326
  74.1 33.4 %collective-permute-start.3 = (bf16[256,1024]{1,0:T(8,128)(2,1)}, bf16[256,1024]{1,0:T(8,128)(2,1)S(1)}, u32[]{:S(2)}, u32[]{:S(2)}) collective-permute-start(bf16[256,1024]{1,0:T(8,128)(2,1)} %slice.11), channel_id=1, source_target_pairs={{0,1},{1,0},{2,3},{3,2},{4,5},{5,4},{6,7},{7,6},{8,9},{9,8},{10,11... | collective-permute-start | bytes 1572872 | tf_op jit(solution)/shard_map/ppermute | solution.py:326
  75.2 23.3 %copy-start.1 = (bf16[1024,3072]{1,0:T(8,128)(2,1)S(1)}, bf16[1024,3072]{1,0:T(8,128)(2,1)}, u32[]{:S(2)}) copy-start(bf16[1024,3072]{1,0:T(8,128)(2,1)} %all-gather.3.cloned.1.call-done.w_ref.refs_1_.refs_3_.refs_2_) | copy-start | bytes 18874372
  98.5 22.8 %collective-permute-start.2 = (bf16[512,1024]{1,0:T(8,128)(2,1)}, bf16[512,1024]{1,0:T(8,128)(2,1)S(1)}, u32[]{:S(2)}, u32[]{:S(2)}) collective-permute-start(bf16[512,1024]{1,0:T(8,128)(2,1)} %collective-permute-done.1.refs_1_), channel_id=1, source_target_pairs={{0,2},{1,31},{2,4},{3,1},{4,6},{5,3},{6,8},{7,5},{8,10},{9,7},{10,... | collective-permute-start | bytes 3145736 | tf_op jit(solution)/shard_map/ppermute | solution.py:300
  107.6 13.7 %collective-permute-start.4 = (bf16[256,1024]{1,0:T(8,128)(2,1)S(1)}, bf16[256,1024]{1,0:T(8,128)(2,1)S(1)}, u32[]{:S(2)}, u32[]{:S(2)}) collective-permute-start(bf16[256,1024]{1,0:T(8,128)(2,1)S(1)} %collective-permute-done.3.refs_2_), channel_id=1, source_target_pairs={{0,2},{1,31},{2,4},{3,1},{4,6},{5,3},{6,8},{7,5},{8,10},{9,7},{10,... | collective-permute-start | bytes 1572872 | tf_op jit(solution)/shard_map/ppermute | solution.py:300
Sparse Core Ops, SparseCore 0:
  9.6 65.4 all-gather.2
  126.2 40.3 all-gather.4
